TPU v7x, 32 devices: a whole 2x2x4 slice. The times are simulated.
32 devices in a mesh: head: 4 (over z), batch: 8 (over y, x, core).
Axes of the slice: x: 2, y: 2, z: 4, core: 2. Of those that a mesh axis runs over, the one named last changes fastest.
Arguments:
- layer_input: bfloat16 [8192, 1024], P(('batch', 'head')), may hold values from -6 to 6
- cotangent: bfloat16 [8192, 1024], P(('batch', 'head')), may hold values from -6 to 6
- segments: int32 [8192], P('batch'), may hold values from 0 to 126, as said below
- mix_gain: float32 [1024], replicated, may hold values from 0.5 to 1.5
- query_weight: bfloat16 [1024, 1024], P('batch', 'head'), may hold values from -0.1875 to 0.1875
- key_weight: bfloat16 [1024, 2048], P('batch', 'head'), may hold values from -0.1875 to 0.1875
- value_weight: bfloat16 [1024, 2048], P('batch', 'head'), may hold values from -0.1875 to 0.1875
- outgate_weight: bfloat16 [1024, 1024], P('batch', 'head'), may hold values from -0.1875 to 0.1875
- rate_weight: bfloat16 [1024, 24], P('batch', 'head'), may hold values from -0.1875 to 0.1875
- conv_query: float32 [4, 1024], replicated, may hold values from -3 to 3
- conv_key: float32 [4, 2048], replicated, may hold values from -3 to 3
- conv_value: float32 [4, 2048], replicated, may hold values from -3 to 3
- decay_bias: float32 [8], replicated, may hold values from -4 to 1
- out_gain: float32 [128], replicated, may hold values from 0.5 to 1.5
- out_weight: bfloat16 [1024, 1024], P('head', 'batch'), may hold values from -0.1875 to 0.1875
- mlp_gain: float32 [1024], replicated, may hold values from 0.5 to 1.5
- gate_weight: bfloat16 [1024, 2816], P('batch', 'head'), may hold values from -0.1875 to 0.1875
- up_weight: bfloat16 [1024, 2816], P('batch', 'head'), may hold values from -0.1875 to 0.1875
- down_weight: bfloat16 [2816, 1024], P('head', 'batch'), may hold values from -0.109375 to 0.109375
Outputs:
- layer_output: bfloat16 [8192, 1024], P(('batch', 'head'))
- input_grad: float32 [8192, 1024], P(('batch', 'head'))
- mix_gain_grad: float32 [1024], replicated
- query_weight_grad: float32 [1024, 1024], P('batch', 'head')
- key_weight_grad: float32 [1024, 2048], P('batch', 'head')
- value_weight_grad: float32 [1024, 2048], P('batch', 'head')
- outgate_weight_grad: float32 [1024, 1024], P('batch', 'head')
- rate_weight_grad: float32 [1024, 24], P('batch', 'head')
- conv_query_grad: float32 [4, 1024], replicated
- conv_key_grad: float32 [4, 2048], replicated
- conv_value_grad: float32 [4, 2048], replicated
- decay_bias_grad: float32 [8], replicated
- out_gain_grad: float32 [128], replicated
- out_weight_grad: float32 [1024, 1024], P('head', 'batch')
- mlp_gain_grad: float32 [1024], replicated
- gate_weight_grad: float32 [1024, 2816], P('batch', 'head')
- up_weight_grad: float32 [1024, 2816], P('batch', 'head')
- down_weight_grad: float32 [2816, 1024], P('head', 'batch')
Inputs may be any that keep to these rules, and one draw needn't show every extreme that they name: `segments`: segment ids count documents within each packed row of 1024 tokens: they are 0 at the row's first token and rise by one at each document's first token; documents begin only before position max(64, 1) or after position 1024 - max(64, 1), so in every row one document covers the positions between; in some row every one of those edge positions begins a document.
All inputs are finite; a program needn't handle non-finite values.
Results may differ from a plain program's by a relative error of at most 0.013.
The roundings to bfloat16 on the way count: a program that leaves them out, or rounds other values in their place, can miss the bound.
Values may be sent and summed in bfloat16 or wider, within the bound.
No kernel may reach another device: no remote copies, remote signals or barrier semaphores. Data moves between devices by JAX's collectives and lax.ppermute only.
A program may use at most 320 MiB of HBM per device.

v0:
```python
from functools import partial

import jax
import jax.numpy as jnp
from jax import lax
from jax.experimental import pallas as pl
from jax.experimental.pallas import tpu as pltpu
from jax.sharding import PartitionSpec as P

HEAD_DIM = 128
EPS = 1e-06
EXACT = lax.Precision.HIGHEST
HIGH = lax.Precision.HIGH
FAST = lax.Precision.DEFAULT
NN = ((1,), (0,))
NT = ((1,), (1,))
TN = ((0,), (0,))
LANE = 128
CHUNK = 64
ROWS = 2 * CHUNK
FWD_CHUNKS = 4
BWD_CHUNKS = 2
SPANS = 2


def mm(left, right, dims=NN, precision=HIGH):
    return lax.dot_general(
        left, right, (dims, ((), ())), precision=precision, preferred_element_type=jnp.float32
    )


def softplus(x):
    return jnp.maximum(x, 0.0) + jnp.log1p(jnp.exp(-jnp.abs(x)))


def chunk_masks():
    row = lax.broadcasted_iota(jnp.int32, (ROWS, ROWS), 0)
    col = lax.broadcasted_iota(jnp.int32, (ROWS, ROWS), 1)
    row_tok, col_tok = row & (CHUNK - 1), col & (CHUNK - 1)
    later = row_tok > col_tok
    same_tok = row_tok == col_tok
    pair = same_tok & (row > col)
    levels = []
    size = 1
    while size < CHUNK:
        upper = (row_tok & size) > (col_tok & size)
        together = (row_tok & (-2 * size)) == (col_tok & (-2 * size))
        levels.append(upper & together)
        size *= 2
    return row, col, later | same_tok, later | pair, pair, levels


def invert(lowers, ident, pair, levels, precision):
    inverses = [ident - jnp.where(pair, lower, 0.0) for lower in lowers]
    for level in levels:
        steps = [
            mm(jnp.where(level, lower, 0.0), inverse, NN, precision)
            for lower, inverse in zip(lowers, inverses)
        ]
        inverses = [
            inverse - mm(inverse, step, NN, precision) for inverse, step in zip(inverses, steps)
        ]
    return inverses


def col_sum(x):
    return jnp.sum(x, axis=-1, keepdims=True)


def twice(x):
    return jnp.concatenate([x, x], axis=0)


def unit_slices(heads, head):
    names = [heads + 2 * head, heads + 2 * head + 1, 3 * heads + 2 * head, 3 * heads + 2 * head + 1]
    names += [head, 5 * heads + head]
    return [slice(n * HEAD_DIM, (n + 1) * HEAD_DIM) for n in names]


def decays_of(cumul, cumul_t, beta_rows, aux, same, lane):
    c_tok = cumul[:, lane + 2 : lane + 3]
    c_end = cumul[CHUNK - 1 :, lane + 2 : lane + 3]
    decay = jnp.where(
        same, jnp.exp(jnp.minimum(twice(c_tok) - cumul_t[lane + 2 : lane + 3, :], 0.0)), 0.0
    )
    beta = jnp.concatenate(
        [beta_rows[:, lane : lane + 1], beta_rows[:, lane + 1 : lane + 2]], axis=0
    )
    start = aux[:, 0:1] * jnp.exp(c_tok)
    final = twice(aux[:, 1:2] * jnp.exp(c_end - c_tok))
    total = aux[CHUNK - 1 :, 0:1] * jnp.exp(c_end)
    return decay, beta, start, final, total


def fwd_kernel(
    heads, per_step, raw_ref, aux_ref, segrow_ref, taps_ref, bias_ref, gain_ref, mem_in, tail_in,
    mixed_ref, pre_ref, recall_ref, inv_ref, prox_ref, state_ref, move_ref, probe_ref,
    mem_ref, tail_ref, act_ref,
):
    width = HEAD_DIM
    block = per_step * CHUNK

    @pl.when(pl.program_id(0) == 0)
    def _():
        mem_ref[...] = mem_in[...]
        tail_ref[...] = tail_in[...]

    masks = [aux_ref[:, 2 + s : 3 + s] for s in range(3)]
    for tile in range(5 * heads):
        cols = slice(tile * width, (tile + 1) * width)
        raw = raw_ref[:, cols]
        joined = jnp.concatenate([tail_ref[:, cols], raw], axis=0)
        pre = raw * taps_ref[0:1, cols]
        for s in range(1, 4):
            shifted = pltpu.roll(joined, s, 0)[8:]
            pre = pre + shifted * masks[s - 1] * taps_ref[s : s + 1, cols]
        pre_ref[:, cols] = pre
        tail_ref[:, cols] = raw[block - 8 :]
        act = pre * jax.nn.sigmoid(pre)
        if tile < 3 * heads:
            act = act * lax.rsqrt(col_sum(act * act) + EPS)
        act_ref[:, cols] = act

    row, col, lower_eq, strict, pair, levels = chunk_masks()
    ident = (row == col).astype(jnp.float32)
    tri = (row[:CHUNK, :CHUNK] >= col[:CHUNK, :CHUNK]).astype(jnp.float32)
    rates = raw_ref[:, 6 * heads * width :]
    beta_tile = jax.nn.sigmoid(rates)
    log_tile = -softplus(rates + bias_ref[...])
    units = [(part, head) for part in range(per_step) for head in range(heads)]
    spans = [slice(part * CHUNK, (part + 1) * CHUNK) for part in range(per_step)]
    cumuls = [mm(tri, log_tile[rows], NN, EXACT) for rows in spans]
    cumul_ts = [twice(cumul).T for cumul in cumuls]
    sames = [
        (twice(aux_ref[rows, 8:9]) == segrow_ref[part]) & lower_eq
        for part, rows in enumerate(spans)
    ]
    keys, queries, decays, lowers, scores = [], [], [], [], []
    for part, head in units:
        k1, k2, v1, v2, q0, g0 = unit_slices(heads, head)
        rows = spans[part]
        key = jnp.concatenate([act_ref[rows, k1], act_ref[rows, k2]], axis=0)
        query = act_ref[rows, q0]
        decay = decays_of(
            cumuls[part], cumul_ts[part], beta_tile[rows], aux_ref[rows], sames[part], 3 * head
        )
        dots = mm(jnp.concatenate([key, query], axis=0), key, NT)
        keys.append(key)
        queries.append(query)
        decays.append(decay)
        lowers.append(jnp.where(strict, decay[1] * decay[0] * dots[:ROWS], 0.0))
        scores.append(decay[0][CHUNK:] * dots[ROWS:])
    inverses = invert(lowers, ident, pair, levels, HIGH)
    solved = []
    for u, (part, head) in enumerate(units):
        k1, k2, v1, v2, q0, g0 = unit_slices(heads, head)
        rows = spans[part]
        decay, beta, start, final, total = decays[u]
        inv_ref[u] = inverses[u]
        value = jnp.concatenate([act_ref[rows, v1], act_ref[rows, v2]], axis=0)
        solved.append(
            mm(
                inverses[u],
                jnp.concatenate([beta * value, beta * twice(start) * keys[u]], axis=1),
            )
        )
    moves = [mm(decays[u][3] * keys[u], solved[u], TN) for u in range(len(units))]
    reads = [mm(scores[u], solved[u]) for u in range(len(units))]
    for u, (part, head) in enumerate(units):
        memory = mem_ref[head]
        state_ref[u] = memory
        move_ref[u] = moves[u][:, width:]
        mem_ref[head] = (
            decays[u][4] * memory + moves[u][:, :width] - mm(moves[u][:, width:], memory)
        )
    for u, (part, head) in enumerate(units):
        probe = decays[u][2] * queries[u] - reads[u][:, width:]
        probe_ref[u] = probe
        seen = mm(jnp.concatenate([solved[u][:, width:], probe], axis=0), state_ref[u])
        prox_ref[u] = solved[u][:, :width] - seen[:ROWS]
        recall = reads[u][:, :width] + seen[ROWS:]
        rows = spans[part]
        cols = slice(head * width, (head + 1) * width)
        recall_ref[rows, cols] = recall
        scale = lax.rsqrt(jnp.mean(recall * recall, axis=-1, keepdims=True) + EPS)
        gate = raw_ref[rows, unit_slices(heads, head)[5]]
        mixed = recall * scale * gain_ref[...] * (gate * jax.nn.sigmoid(gate))
        mixed_ref[rows, cols] = mixed.astype(jnp.bfloat16)


def bwd_kernel(
    heads, per_step, grad_ref, raw_ref, aux_ref, segrow_ref, pre_ref, recall_ref, inv_ref,
    prox_ref, state_ref, move_ref, probe_ref, taps_ref, bias_ref, gain_ref,
    adj_in, head_in, taps_grad_in, bias_grad_in, gain_grad_in, low_in,
    low_ref, taps_grad_ref, bias_grad_ref, gain_grad_ref, adj_ref, head_ref,
    act_ref, norm_ref, dact_ref, keep_ref,
):
    width = HEAD_DIM
    block = per_step * CHUNK

    @pl.when(pl.program_id(0) == 0)
    def _():
        adj_ref[...] = adj_in[...]
        head_ref[...] = head_in[...]
        taps_grad_ref[...] = taps_grad_in[...]
        bias_grad_ref[...] = bias_grad_in[...]
        gain_grad_ref[...] = gain_grad_in[...]

    row, col, lower_eq, strict, pair, levels = chunk_masks()
    tri = (row[:CHUNK, :CHUNK] >= col[:CHUNK, :CHUNK]).astype(jnp.float32)
    tri_t = (row[:CHUNK, :CHUNK] <= col[:CHUNK, :CHUNK]).astype(jnp.float32)
    lanes = col[:CHUNK, :]
    rates = raw_ref[:, 6 * heads * width :]
    beta_tile = jax.nn.sigmoid(rates)
    keep_in = rates + bias_ref[...]
    log_tile = -softplus(keep_in)
    units = [(part, head) for part in reversed(range(per_step)) for head in range(heads)]
    spans = [slice(part * CHUNK, (part + 1) * CHUNK) for part in range(per_step)]
    cumuls = [mm(tri, log_tile[rows], NN, EXACT) for rows in spans]
    cumul_ts = [twice(cumul).T for cumul in cumuls]
    sames = [
        (twice(aux_ref[rows, 8:9]) == segrow_ref[part]) & lower_eq
        for part, rows in enumerate(spans)
    ]
    gain_total = jnp.zeros((1, width), jnp.float32)
    out_grads = []
    for part, head in units:
        rows = spans[part]
        q0, g0 = unit_slices(heads, head)[4:]
        recall = recall_ref[rows, q0]
        grad = grad_ref[rows, q0].astype(jnp.float32)
        gate = raw_ref[rows, g0]
        gate_sig = jax.nn.sigmoid(gate)
        silu_gate = gate * gate_sig
        scale = lax.rsqrt(jnp.mean(recall * recall, axis=-1, keepdims=True) + EPS)
        normed = recall * scale
        gain_total = gain_total + jnp.sum(grad * normed * silu_gate, axis=0, keepdims=True)
        weighted = grad * gain_ref[...]
        low_ref[rows, g0] = (
            weighted * normed * gate_sig * (1.0 + gate * (1.0 - gate_sig))
        ).astype(jnp.bfloat16)
        normed_grad = weighted * silu_gate
        out_grads.append(
            scale * (normed_grad - normed * jnp.mean(normed_grad * normed, axis=-1, keepdims=True))
        )
    gain_grad_ref[...] += gain_total
    reads = [
        mm(probe_ref[part * heads + head], out_grads[u], TN) for u, (part, head) in enumerate(units)
    ]
    for u, (part, head) in enumerate(units):
        spot = part * heads + head
        c_end = cumuls[part][CHUNK - 1 :, 3 * head + 2 : 3 * head + 3]
        total = aux_ref[(part + 1) * CHUNK - 1 : (part + 1) * CHUNK, 0:1] * jnp.exp(c_end)
        adjoint = adj_ref[head]
        keep_ref[spot] = adjoint
        adj_ref[head] = total * adjoint + reads[u] - mm(move_ref[spot], adjoint, TN)
    for tile in range(5 * heads):
        cols = slice(tile * width, (tile + 1) * width)
        pre = pre_ref[:, cols]
        act = pre * jax.nn.sigmoid(pre)
        if tile < 3 * heads:
            scale = lax.rsqrt(col_sum(act * act) + EPS)
            norm_ref[:, cols] = jnp.broadcast_to(scale, act.shape)
            act = act * scale
        act_ref[:, cols] = act
    keys, decays, dots = [], [], []
    for u, (part, head) in enumerate(units):
        k1, k2, v1, v2, q0, g0 = unit_slices(heads, head)
        rows = spans[part]
        key = jnp.concatenate([act_ref[rows, k1], act_ref[rows, k2]], axis=0)
        keys.append(key)
        decays.append(
            decays_of(
                cumuls[part], cumul_ts[part], beta_tile[rows], aux_ref[rows], sames[part], 3 * head
            )
        )
        dots.append(mm(jnp.concatenate([key, act_ref[rows, q0]], axis=0), key, NT))
    scores = [decays[u][0][CHUNK:] * dots[u][ROWS:] for u in range(len(units))]
    proxy_grads = [
        mm(scores[u], out_grads[u], TN)
        + mm(decays[u][3] * keys[u], keep_ref[part * heads + head])
        for u, (part, head) in enumerate(units)
    ]
    both_grads = [
        jnp.concatenate(
            [mm(inv_ref[part * heads + head], proxy_grads[u], TN), out_grads[u]], axis=0
        )
        for u, (part, head) in enumerate(units)
    ]
    outers = [
        mm(both_grads[u], prox_ref[part * heads + head], NT)
        for u, (part, head) in enumerate(units)
    ]
    throughs = [
        mm(both_grads[u], state_ref[part * heads + head], NT)
        for u, (part, head) in enumerate(units)
    ]
    finals = [
        decays[u][3] * mm(prox_ref[part * heads + head], keep_ref[part * heads + head], NT)
        for u, (part, head) in enumerate(units)
    ]
    score_grads, inners, beta_parts, log_cols = [], [], [], []
    for u, (part, head) in enumerate(units):
        decay, beta, start, final, total = decays[u]
        key_decay = jnp.where(strict, decay * dots[u][:ROWS], 0.0)
        lower_grad = -outers[u][:ROWS]
        beta_part = lower_grad * key_decay
        dots_grad = jnp.where(strict, lower_grad * beta * decay, 0.0)
        score_grad = outers[u][ROWS:] * decay[CHUNK:]
        log_part = beta_part * beta
        log_part = jnp.concatenate(
            [log_part[:CHUNK], log_part[CHUNK:] + outers[u][ROWS:] * scores[u]], axis=0
        )
        log_cols.append(col_sum(log_part - log_part.T))
        beta_parts.append(col_sum(beta_part))
        score_grads.append(score_grad)
        inners.append(
            mm(jnp.concatenate([dots_grad + dots_grad.T, score_grad], axis=0), keys[u])
        )
    zero = jnp.zeros((CHUNK, width), jnp.float32)
    beta_grads, cumul_grads, end_grads = [zero] * per_step, [zero] * per_step, [zero] * per_step
    for u, (part, head) in enumerate(units):
        k1, k2, v1, v2, q0, g0 = unit_slices(heads, head)
        rows = spans[part]
        spot = part * heads + head
        lane = 3 * head
        decay, beta, start, final, total = decays[u]
        through, final_part, right_grad = throughs[u], finals[u], both_grads[u][:ROWS]
        query = act_ref[rows, q0]
        value = jnp.concatenate([act_ref[rows, v1], act_ref[rows, v2]], axis=0)
        beta_start = beta * twice(start)
        key_through = col_sum(keys[u] * through[:ROWS])
        query_through = start * col_sum(query * through[ROWS:])
        final_sum = col_sum(keys[u] * final_part)
        key_grad = (
            inners[u][:ROWS]
            + mm(score_grads[u], query, TN)
            - beta_start * through[:ROWS]
            + final_part
        )
        dact_ref[rows, k1] = key_grad[:CHUNK]
        dact_ref[rows, k2] = key_grad[CHUNK:]
        value_grad = beta * right_grad
        dact_ref[rows, v1] = value_grad[:CHUNK]
        dact_ref[rows, v2] = value_grad[CHUNK:]
        dact_ref[rows, q0] = inners[u][ROWS:] + start * through[ROWS:]
        beta_col = col_sum(right_grad * value) - twice(start) * key_through + beta_parts[u]
        c_grad = log_cols[u] - beta_start * key_through - final_sum
        c_grad = c_grad[:CHUNK] + c_grad[CHUNK:] + query_through
        end_part = jnp.sum(final_sum, axis=0, keepdims=True) + total * jnp.sum(
            col_sum(state_ref[spot] * keep_ref[spot]), axis=0, keepdims=True
        )
        beta_grads[part] = jnp.where(
            lanes == lane,
            beta_col[:CHUNK],
            jnp.where(lanes == lane + 1, beta_col[CHUNK:], beta_grads[part]),
        )
        cumul_grads[part] = jnp.where(lanes == lane + 2, c_grad, cumul_grads[part])
        end_grads[part] = jnp.where(lanes == lane + 2, end_part, end_grads[part])
    bias_total = jnp.zeros((1, width), jnp.float32)
    for part, rows in enumerate(spans):
        log_grad = mm(tri_t, cumul_grads[part], NN, EXACT) + end_grads[part]
        beta_rows = beta_tile[rows]
        keep_grad = -log_grad * jax.nn.sigmoid(keep_in[rows]) * aux_ref[rows, 2:3]
        rate_grad = beta_grads[part] * beta_rows * (1.0 - beta_rows) + keep_grad
        bias_total = bias_total + jnp.sum(keep_grad, axis=0, keepdims=True)
        low_ref[rows, 6 * heads * width :] = rate_grad.astype(jnp.bfloat16)
    bias_grad_ref[...] += bias_total

    masks = [aux_ref[:, 5 + s : 6 + s] for s in range(3)]
    for tile in range(5 * heads):
        cols = slice(tile * width, (tile + 1) * width)
        pre = pre_ref[:, cols]
        sig = jax.nn.sigmoid(pre)
        grad = dact_ref[:, cols]
        if tile < 3 * heads:
            act = act_ref[:, cols]
            grad = norm_ref[:, cols] * (grad - act * col_sum(grad * act))
        grad = grad * sig * (1.0 + pre * (1.0 - sig))
        raw = raw_ref[:, cols]
        joined = jnp.concatenate([grad, head_ref[:, cols]], axis=0)
        head_ref[:, cols] = grad[:8]
        raw_grad = grad * taps_ref[0:1, cols]
        taps_grad_ref[0:1, cols] += jnp.sum(raw * grad, axis=0, keepdims=True)
        for s in range(1, 4):
            shifted = pltpu.roll(joined, block + 8 - s, 0)[:block] * masks[s - 1]
            raw_grad = raw_grad + shifted * taps_ref[s : s + 1, cols]
            taps_grad_ref[s : s + 1, cols] += jnp.sum(raw * shifted, axis=0, keepdims=True)
        low_ref[:, cols] = raw_grad.astype(jnp.bfloat16)


def token_aux(segments):
    length = segments.shape[0]
    seg = segments.astype(jnp.int32)
    chunks = seg.reshape(length // CHUNK, CHUNK)
    last = chunks[:, -1]
    before = jnp.concatenate([jnp.full((1,), -1, jnp.int32), last[:-1]])
    columns = [
        (chunks == before[:, None]).reshape(length),
        (chunks == last[:, None]).reshape(length),
    ]
    for s in range(1, 4):
        columns.append(jnp.pad(seg, (s, 0), constant_values=-1)[:length] == seg)
    for s in range(1, 4):
        columns.append(jnp.pad(seg, (0, s), constant_values=-1)[s:] == seg)
    columns.append(seg)
    columns += [jnp.zeros_like(seg)] * 7
    aux = jnp.stack([c.astype(jnp.float32) for c in columns], axis=1)
    row = chunks.astype(jnp.float32)
    return aux, jnp.concatenate([row, row], axis=1)[:, None, :]


def kernel_params():
    return pltpu.CompilerParams(
        dimension_semantics=("arbitrary",), vmem_limit_bytes=48 * 1024 * 1024
    )


def pin(array):
    return pltpu.with_memory_space_constraint(array, pltpu.HBM)


def whole(shape):
    zeros = (0,) * len(shape)
    return pl.BlockSpec(shape, lambda i: zeros)


def mixer_forward(raw, aux, segrow, taps, bias, gain, carry, heads, per_step, part, parts):
    width = HEAD_DIM
    block = per_step * CHUNK
    length = raw.shape[0] // parts
    steps = length // block
    first = part * steps
    units = per_step * heads
    total_units = steps * units
    cols = raw.shape[1]
    f32 = jnp.float32
    if carry is None:
        carry = (jnp.zeros((heads, width, width), f32), jnp.zeros((8, 5 * heads * width), f32))
    memory, tail = carry
    read = lambda i: (first + i, 0)
    read_cube = lambda i: (first + i, 0, 0)
    tiles = lambda i: (i, 0)
    cubes = lambda i: (i, 0, 0)
    unit_spec = pl.BlockSpec((units, ROWS, width), cubes)
    unit_shape = pltpu.HBM((total_units, ROWS, width), f32)
    out = pl.pallas_call(
        partial(fwd_kernel, heads, per_step),
        grid=(steps,),
        in_specs=[
            pl.BlockSpec((block, cols), read),
            pl.BlockSpec((block, 16), read),
            pl.BlockSpec((per_step, 1, ROWS), read_cube),
            whole(taps.shape),
            whole((1, width)),
            whole((1, width)),
            whole(memory.shape),
            whole(tail.shape),
        ],
        out_specs=[
            pl.BlockSpec((block, heads * width), tiles),
            pl.BlockSpec((block, 5 * heads * width), tiles),
            pl.BlockSpec((block, heads * width), tiles),
            unit_spec,
            unit_spec,
            unit_spec,
            unit_spec,
            pl.BlockSpec((units, CHUNK, width), cubes),
            whole(memory.shape),
            whole(tail.shape),
        ],
        out_shape=[
            jax.ShapeDtypeStruct((length, heads * width), jnp.bfloat16),
            pltpu.HBM((length, 5 * heads * width), f32),
            pltpu.HBM((length, heads * width), f32),
            unit_shape,
            unit_shape,
            unit_shape,
            unit_shape,
            pltpu.HBM((total_units, CHUNK, width), f32),
            jax.ShapeDtypeStruct(memory.shape, f32),
            jax.ShapeDtypeStruct(tail.shape, f32),
        ],
        scratch_shapes=[pltpu.VMEM((block, 5 * heads * width), f32)],
        compiler_params=kernel_params(),
        name="mixer_forward",
    )(raw, aux, segrow, taps, bias, gain, memory, tail)
    return out[0], out[1:8], (out[8], out[9])


def mixer_backward(grad, raw, aux, segrow, saved, taps, bias, gain, carry, heads, per_step, part, parts):
    width = HEAD_DIM
    block = per_step * CHUNK
    length = raw.shape[0] // parts
    steps = length // block
    last = (part + 1) * steps - 1
    units = per_step * heads
    cols = raw.shape[1]
    f32 = jnp.float32
    shapes = [
        (heads, width, width),
        (8, 5 * heads * width),
        taps.shape,
        (1, width),
        (1, width),
    ]
    low_shape = pltpu.HBM(raw.shape, jnp.bfloat16)
    if carry is None:
        carry = [jnp.zeros(shape, f32) for shape in shapes] + [jnp.zeros((16, width), jnp.bfloat16)]
        aliases = {}
    else:
        aliases = {19: 0}
    read = lambda i: (last - i, 0)
    read_cube = lambda i: (last - i, 0, 0)
    tiles = lambda i: (steps - 1 - i, 0)
    cubes = lambda i: (steps - 1 - i, 0, 0)
    unit_spec = pl.BlockSpec((units, ROWS, width), cubes)
    out = pl.pallas_call(
        partial(bwd_kernel, heads, per_step),
        grid=(steps,),
        in_specs=[
            pl.BlockSpec((block, heads * width), read),
            pl.BlockSpec((block, cols), read),
            pl.BlockSpec((block, 16), read),
            pl.BlockSpec((per_step, 1, ROWS), read_cube),
            pl.BlockSpec((block, 5 * heads * width), tiles),
            pl.BlockSpec((block, heads * width), tiles),
            unit_spec,
            unit_spec,
            unit_spec,
            unit_spec,
            pl.BlockSpec((units, CHUNK, width), cubes),
            whole(taps.shape),
            whole((1, width)),
            whole((1, width)),
        ]
        + [whole(shape) for shape in shapes]
        + [pl.BlockSpec(memory_space=pl.ANY)],
        out_specs=[
            pl.BlockSpec((block, cols), read),
            whole(taps.shape),
            whole((1, width)),
            whole((1, width)),
            whole(shapes[0]),
            whole(shapes[1]),
        ],
        out_shape=[
            low_shape,
            jax.ShapeDtypeStruct(taps.shape, f32),
            jax.ShapeDtypeStruct((1, width), f32),
            jax.ShapeDtypeStruct((1, width), f32),
            jax.ShapeDtypeStruct(shapes[0], f32),
            jax.ShapeDtypeStruct(shapes[1], f32),
        ],
        scratch_shapes=[
            pltpu.VMEM((block, 5 * heads * width), f32),
            pltpu.VMEM((block, 3 * heads * width), f32),
            pltpu.VMEM((block, 5 * heads * width), f32),
            pltpu.VMEM((units, width, width), f32),
        ],
        input_output_aliases=aliases,
        compiler_params=kernel_params(),
        name="mixer_backward",
    )(grad, raw, aux, segrow, *[pin(array) for array in saved], taps, bias, gain, *carry)
    low, taps_grad, bias_grad, gain_grad, adjoint, head = out
    return [adjoint, head, taps_grad, bias_grad, gain_grad, low]


def up_to(x, multiple):
    return -(-x // multiple) * multiple


def row_scale(values):
    return lax.rsqrt(jnp.mean(values * values, axis=-1, keepdims=True) + EPS)


def norm_back(grad, values, scale, gain):
    normed = values * scale
    gain_grad = jnp.sum(grad * normed, axis=0)
    weighted = grad * gain
    value_grad = scale * (weighted - normed * jnp.mean(weighted * normed, axis=-1, keepdims=True))
    return (value_grad, gain_grad)


def dot(left, right, dims=NN):
    return lax.dot_general(left, right, (dims, ((), ())), preferred_element_type=jnp.float32)


def swap(x, axis, bit):
    size = lax.axis_size(axis)
    return lax.ppermute(x, axis, [(i, i ^ bit) for i in range(size)])


def exchange(blocks, axis):
    return lax.all_to_all(blocks, axis, split_axis=0, concat_axis=0, tiled=True)


def trade(blocks, axis):
    return [blocks[0]] + [swap(block, axis, r) for r, block in enumerate(blocks) if r > 0]


def rows_of(array, index, rows):
    return lax.dynamic_slice_in_dim(array, index * rows, rows, axis=0)


def in_order(blocks, index):
    rows = blocks[0].shape[0]
    out = jnp.zeros((rows * len(blocks),) + blocks[0].shape[1:], blocks[0].dtype)
    for r, block in enumerate(blocks):
        out = lax.dynamic_update_slice_in_dim(out, block, (index ^ r) * rows, axis=0)
    return out


def bits_of(size):
    return [1 << b for b in range(size.bit_length() - 1)]


def chip_sum(left, right, axis):
    size = lax.axis_size(axis)
    core = lax.axis_index(axis) % 2
    width = left.shape[1] // size
    even = jnp.concatenate(
        [left[:, j * width : (j + 1) * width] for j in range(0, size, 2)], axis=1
    )
    odd = jnp.concatenate([left[:, j * width : (j + 1) * width] for j in range(1, size, 2)], axis=1)
    got = swap(dot(jnp.where(core == 0, odd, even), right, TN).astype(jnp.bfloat16), axis, 1)
    held = dot(jnp.where(core == 0, even, odd), right, TN) + got.astype(jnp.float32)
    return held.astype(jnp.bfloat16)


def plane_scatter(held, axis):
    chips = lax.axis_size(axis) // 2
    chip = lax.axis_index(axis) // 2
    width = held.shape[0] // chips
    total = rows_of(held, chip, width).astype(jnp.float32)
    for step in range(1, chips):
        total = total + swap(rows_of(held, chip ^ step, width), axis, 2 * step).astype(jnp.float32)
    return total


def body(
    layer_input,
    cotangent,
    segments,
    mix_gain,
    query_weight,
    key_weight,
    value_weight,
    outgate_weight,
    rate_weight,
    conv_query,
    conv_key,
    conv_value,
    decay_bias,
    out_gain,
    out_weight,
    mlp_gain,
    gate_weight,
    up_weight,
    down_weight,
):
    f32, bf16 = jnp.float32, jnp.bfloat16
    head_index = lax.axis_index("head")
    n_head, n_batch = lax.axis_size("head"), lax.axis_size("batch")
    rows, width = layer_input.shape
    length = rows * n_head
    local_heads = query_weight.shape[1] // HEAD_DIM
    unit = local_heads * HEAD_DIM
    mix_cols = 6 * unit + HEAD_DIM
    ff = gate_weight.shape[1]
    ff_pad = up_to(ff, LANE)

    copies = jnp.broadcast_to(layer_input[None], (n_head,) + layer_input.shape)
    copies, query_weight, key_weight, value_weight, outgate_weight = lax.optimization_barrier(
        (copies, query_weight, key_weight, value_weight, outgate_weight)
    )
    tokens = exchange(copies, "head")
    own_mix = jnp.concatenate(
        [
            query_weight,
            key_weight,
            value_weight,
            outgate_weight,
            jnp.pad(rate_weight, ((0, 0), (0, HEAD_DIM - rate_weight.shape[1]))),
        ],
        axis=1,
    )
    proj_w = lax.all_gather(own_mix, "batch", axis=0, tiled=True)

    pad = ((0, 0), (0, ff_pad - ff))
    own_ff = jnp.concatenate(
        [jnp.pad(gate_weight, pad), jnp.pad(up_weight, pad), jnp.pad(down_weight.T, pad)], axis=1
    )
    ff_sets = [lax.all_gather(own_ff, "batch", axis=0, tiled=True)]
    def head_cols(table, per_head):
        return lax.dynamic_slice_in_dim(
            table, head_index * local_heads * per_head, local_heads * per_head, axis=table.ndim - 1
        )

    taps = jnp.concatenate(
        [
            head_cols(conv_query, HEAD_DIM),
            head_cols(conv_key, 2 * HEAD_DIM),
            head_cols(conv_value, 2 * HEAD_DIM),
        ],
        axis=1,
    )
    own_bias = head_cols(decay_bias, 1)
    bias = jnp.stack([jnp.zeros_like(own_bias), jnp.zeros_like(own_bias), own_bias], axis=1)
    bias = jnp.pad(bias.reshape(-1), (0, HEAD_DIM - 3 * local_heads))[None]
    aux, segrow = token_aux(segments)
    tokens, later_ff, later_out, later_cot, aux, segrow, taps, bias = lax.optimization_barrier(
        (tokens, own_ff, out_weight.T, cotangent, aux, segrow, taps, bias)
    )
    out_shards = trade([later_out] * n_head, "head")
    shards = [later_ff]
    for bit in bits_of(n_head)[1:]:
        shards = shards + [swap(shard, "head", bit) for shard in shards]
    pair_grad = swap(later_cot, "head", 1)

    all_in = tokens.reshape(length, width).astype(f32)
    scale_all = row_scale(all_in)
    rows_in = (all_in * scale_all * mix_gain).astype(bf16)
    rows_in, out_shards = lax.optimization_barrier((rows_in, out_shards))
    out_all = lax.all_gather(
        jnp.concatenate(out_shards, axis=1), "batch", axis=0, tiled=True
    )
    raw, ff_sets[0] = lax.optimization_barrier((dot(rows_in, proj_w), ff_sets[0]))

    gain = out_gain[None]
    consts = (raw, aux, segrow, taps, bias, gain)
    carry, mixed_parts, saved = None, [], []
    for part in range(SPANS):
        if part == SPANS - 1:
            carry, shards = lax.optimization_barrier((carry, shards))
        mixed_part, kept, carry = mixer_forward(*consts, carry, local_heads, FWD_CHUNKS, part, SPANS)
        mixed_parts.append(mixed_part)
        saved.append(kept)
    mixed_parts, pair_grad = lax.optimization_barrier((mixed_parts, pair_grad))
    mixed_low = jnp.concatenate(mixed_parts, axis=0)
    ff_sets += [lax.all_gather(shard, "batch", axis=0, tiled=True) for shard in shards[1:]]

    mixed_all = jnp.concatenate(
        trade([rows_of(mixed_low, head_index ^ r, rows) for r in range(n_head)], "head"), axis=1
    )
    resid_in = layer_input.astype(f32)
    resid_mid = resid_in + dot(mixed_all, out_all, NT)
    scale_mid = row_scale(resid_mid)
    normed_mid = (resid_mid * scale_mid * mlp_gain).astype(bf16)
    pair_mid = swap(normed_mid, "head", 1)

    def feed_forward(mid, cot):
        mid_part = None
        grads = []
        for ff_set in ff_sets:
            gate_up = dot(mid, ff_set[:, : 2 * ff_pad])
            gate_pre, up_pre = gate_up[:, :ff_pad], gate_up[:, ff_pad:]
            gate_sig = jax.nn.sigmoid(gate_pre)
            silu_gate = gate_pre * gate_sig
            hidden = (silu_gate * up_pre).astype(bf16)
            hidden_grad = dot(cot, ff_set[:, 2 * ff_pad : 3 * ff_pad])
            gate_grad = (
                hidden_grad * up_pre * gate_sig * (1.0 + gate_pre * (1.0 - gate_sig))
            ).astype(bf16)
            up_grad = (hidden_grad * silu_gate).astype(bf16)
            both_grad = jnp.concatenate([gate_grad, up_grad], axis=1)
            mid_here = dot(both_grad, ff_set[:, : 2 * ff_pad], NT)
            mid_part = mid_here if mid_part is None else mid_part + mid_here
            grads.append((both_grad, hidden))
        return mid_part, grads

    mid_own, grads_own = feed_forward(normed_mid, cotangent)
    pair_mid, grads_own[0] = lax.optimization_barrier((pair_mid, grads_own[0]))
    mid_pair, grads_pair = feed_forward(pair_mid, pair_grad)
    both_mid = jnp.concatenate([normed_mid, pair_mid], axis=0)
    both_cot = jnp.concatenate([cotangent, pair_grad], axis=0)

    def weight_sums(mid, cot, own, pair):
        both, hidden = [jnp.concatenate(pieces, axis=0) for pieces in zip(own, pair)]
        return jnp.concatenate([dot(mid, both, TN), dot(cot, hidden, TN)], axis=1).astype(bf16)

    half = len(ff_sets) // 2
    ff_grads = list(zip(grads_own, grads_pair))
    ff_first = [weight_sums(both_mid, both_cot, *grads) for grads in reversed(ff_grads[half:])]
    mid_swap, ff_first, mid_own = lax.optimization_barrier(
        (swap(mid_pair.astype(bf16), "head", 1), ff_first, mid_own)
    )
    mid_grad = mid_own + mid_swap.astype(f32)
    mid_back, mlp_gain_part = norm_back(mid_grad, resid_mid, scale_mid, mlp_gain)
    resid_grad = cotangent.astype(f32) + mid_back
    branch_grad = resid_grad.astype(bf16)
    mixed_grad = dot(branch_grad, out_all).astype(bf16)
    mixed_grad = trade([mixed_grad[:, r * unit : (r + 1) * unit] for r in range(n_head)], "head")
    mixed_grad[1], out_hidden = lax.optimization_barrier(
        (mixed_grad[1], [hidden for _, hidden in grads_pair])
    )
    mixed_grad = in_order(mixed_grad, head_index)
    ff_first = [
        lax.psum_scatter(part, "batch", scatter_dimension=0, tiled=True) for part in ff_first
    ]
    downs = [ff_set[:, 2 * ff_pad : 3 * ff_pad] for ff_set in ff_sets]
    out_pair = sum(dot(hidden, down, NT) for hidden, down in zip(out_hidden, downs))
    out_swap = swap(out_pair.astype(bf16), "head", 1)

    carry = None
    for part in reversed(range(SPANS)):
        if part == 0:
            carry, branch_rows, both_mid, both_cot, ff_grads = lax.optimization_barrier(
                (carry, branch_grad, both_mid, both_cot, ff_grads[:half])
            )
            ff_last = [weight_sums(both_mid, both_cot, *grads) for grads in reversed(ff_grads)]
            ff_last[-1] = jnp.concatenate(
                [ff_last[-1], dot(branch_rows.T, mixed_all).astype(bf16)], axis=1
            )
            carry, _, ff_first = lax.optimization_barrier((carry, ff_last, ff_first))
            ff_last = [
                lax.psum_scatter(rest, "batch", scatter_dimension=0, tiled=True)
                for rest in ff_last
            ]
        carry = mixer_backward(
            mixed_grad, raw, aux, segrow, saved[part], taps, bias, gain, carry,
            local_heads, BWD_CHUNKS, part, SPANS,
        )
    _, _, taps_grad, bias_grad, gain_grad, raw_low = carry
    raw_low, taps_grad, bias_grad, gain_grad, out_swap, sent = lax.optimization_barrier(
        (
            raw_low,
            taps_grad,
            bias_grad,
            gain_grad,
            out_swap,
            [swap(part, "head", bits_of(n_head)[-1]) for part in ff_first],
        )
    )
    total = dot(raw_low, proj_w, NT).astype(bf16)
    total, later_low = lax.optimization_barrier((total, raw_low))
    received = exchange(total.reshape(n_head, rows, width), "head")
    held = chip_sum(rows_in, later_low, "batch")
    mix_rows, late_tokens, late_scale, held = lax.optimization_barrier(
        (total, tokens, scale_all, held)
    )
    normed_all = late_tokens.reshape(length, width).astype(f32) * late_scale
    mix_gain_part = jnp.sum(mix_rows.astype(f32) * normed_all, axis=0)
    mix_total = plane_scatter(held, "batch")
    hiddens, _ = lax.optimization_barrier(([hidden for _, hidden in grads_own], held))
    out_own = sum(dot(own, down, NT) for own, down in zip(hiddens, downs))
    layer_output = (resid_mid + out_own + out_swap.astype(f32)).astype(bf16)
    ff_kept, _ = lax.optimization_barrier((ff_last, held))
    ff_total = [got.astype(f32) + kept.astype(f32) for got, kept in zip(sent, [kept[:, : 3 * ff_pad] for kept in ff_kept])]
    for bit in reversed(bits_of(n_head)[1:-1]):
        half = len(ff_total) // 2
        ff_total = [
            kept + swap(part.astype(bf16), "head", bit).astype(f32)
            for part, kept in zip(ff_total[:half], ff_total[half:])
        ]
    ff_total = ff_total[0].T
    done = (
        layer_output,
        mix_total[:, :unit],
        mix_total[:, unit : 3 * unit],
        mix_total[:, 3 * unit : 5 * unit],
        mix_total[:, 5 * unit : 6 * unit],
        mix_total[:, 6 * unit : 6 * unit + rate_weight.shape[1]],
        ff_total[:ff].T,
        ff_total[ff_pad : ff_pad + ff].T,
        ff_total[2 * ff_pad : 2 * ff_pad + ff],
    )

    own_bias_grad = bias_grad[0, : 3 * local_heads].reshape(local_heads, 3)[:, 2]
    small = [
        taps_grad[:, :unit].reshape(-1),
        taps_grad[:, unit : 3 * unit].reshape(-1),
        taps_grad[:, 3 * unit :].reshape(-1),
        own_bias_grad,
        gain_grad[0],
        mlp_gain_part,
        mix_gain_part,
    ]
    lengths = [part.shape[0] for part in small]
    packed, mix_total, out_sum = lax.optimization_barrier(
        (pack(small), mix_total, ff_kept[-1][:, 3 * ff_pad :])
    )
    out_blocks = trade([out_sum[:, r * unit : (r + 1) * unit] for r in range(n_head)], "head")
    for bit in bits_of(n_batch):
        packed = packed + swap(packed, "batch", bit)
    small = unpack(packed, lengths)

    def place_cols(table_shape, local_part, per_head):
        local_part = local_part.reshape(table_shape[:-1] + (-1,))
        return lax.dynamic_update_slice_in_dim(
            jnp.zeros(table_shape, f32),
            local_part,
            head_index * local_heads * per_head,
            axis=len(table_shape) - 1,
        ).reshape(-1)

    tables = [
        place_cols(conv_query.shape, small[0], HEAD_DIM),
        place_cols(conv_key.shape, small[1], 2 * HEAD_DIM),
        place_cols(conv_value.shape, small[2], 2 * HEAD_DIM),
        place_cols(decay_bias.shape, small[3], 1),
    ] + small[4:]
    lengths = [part.shape[0] for part in tables]
    packed, received, done = lax.optimization_barrier((pack(tables), received, done))
    for bit in bits_of(n_head):
        packed = packed + swap(packed, "head", bit)
    tables = unpack(packed, lengths)
    in_grad = jnp.sum(received.astype(f32), axis=0)
    in_back, _ = norm_back(in_grad, resid_in, row_scale(resid_in), mix_gain)
    input_grad = resid_grad + in_back

    out_total = sum(block.astype(f32) for block in out_blocks)
    return (
        done[0],
        input_grad,
        tables[6],
        *done[1:6],
        tables[0].reshape(conv_query.shape),
        tables[1].reshape(conv_key.shape),
        tables[2].reshape(conv_value.shape),
        tables[3],
        tables[4],
        out_total.T,
        tables[5],
        *done[6:],
    )


def pack(parts):
    flat = jnp.concatenate(parts)
    return jnp.pad(flat, (0, -flat.shape[0] % (8 * LANE))).reshape(-1, LANE)


def unpack(packed, lengths):
    flat = packed.reshape(-1)
    out, at = [], 0
    for size in lengths:
        out.append(flat[at : at + size])
        at += size
    return out


def solution(mesh):
    placed = (
        P(("batch", "head"), None),
        P(("batch", "head"), None),
        P("batch"),
        P(),
        P("batch", "head"),
        P("batch", "head"),
        P("batch", "head"),
        P("batch", "head"),
        P("batch", "head"),
        P(),
        P(),
        P(),
        P(),
        P(),
        P("head", "batch"),
        P(),
        P("batch", "head"),
        P("batch", "head"),
        P("head", "batch"),
    )
    return jax.shard_map(
        body,
        mesh=mesh,
        in_specs=placed,
        out_specs=(
            P(("batch", "head"), None),
            P(("batch", "head"), None),
            P(),
            P("batch", "head"),
            P("batch", "head"),
            P("batch", "head"),
            P("batch", "head"),
            P("batch", "head"),
            P(),
            P(),
            P(),
            P(),
            P(),
            P("head", "batch"),
            P(),
            P("batch", "head"),
            P("batch", "head"),
            P("head", "batch"),
        ),
        check_vma=False,
    )
```

profile of v0, /device:TPU:0, one launch (start us, length us, event | category | flops | bytes accessed | tf_op | source)
XLA Modules:
  0.0 364.2 jit_solution(11232499407340789582)
XLA Ops:
  7.3 2.8 broadcast_in_dim.18
  12.2 6.5 %all-to-all-start = ((bf16[4,256,1024]{2,1,0:T(8,128)(2,1)}), bf16[4,256,1024]{2,1,0:T(8,128)(2,1)S(1)}, u32[]{:S(2)}, u32[]{:S(2)}) async-start(bf16[4,256,1024]{2,1,0:T(8,128)(2,1)} %broadcast_in_dim.18), calls=%async_computation | async-start | bytes 4194304 | tf_op jit(solution)/shard_map/all_to_all | solution.py:595
  20.9 46.0 %all-to-all-done = bf16[4,256,1024]{2,1,0:T(8,128)(2,1)S(1)} async-done(((bf16[4,256,1024]{2,1,0:T(8,128)(2,1)}), bf16[4,256,1024]{2,1,0:T(8,128)(2,1)S(1)}, u32[]{:S(2)}, u32[]{:S(2)}) %all-to-all-start) | async-done | bytes 2097184 | tf_op jit(solution)/shard_map/all_to_all | solution.py:595
  76.6 9.3 %fusion.125.raw_ref = f32[1024,1664]{1,0:T(8,128)} fusion(bf16[1024,1024]{1,0:T(8,128)(2,1)} %fusion.3, bf16[1024,1664]{1,0:T(8,128)(2,1)} %all-gather.5.cloned.1.call-done), kind=kOutput, calls=%fused_computation.231 | convolution fusion | flops 3489660928 | bytes 12320768 | tf_op jit(solution)/shard_map/dot_general | solution.py:586
  85.9 3.3 all-gather.7.cloned.1.call-done
  89.2 16.5 %mixer_forward.2 = (bf16[512,256]{1,0:T(8,128)(2,1)S(1)}, f32[512,1280]{1,0:T(8,128)}, f32[512,256]{1,0:T(8,128)}, f32[16,128,128]{2,1,0:T(8,128)}, f32[16,128,1...) custom-call(f32[1024,1664]{1,0:T(8,128)} %fusion.125.raw_ref, ...), custom_call_target="tpu_custom_call" | custom-call | tf_op jit(solution)/shard_map/mixer_forward/pallas_call | solution.py:447
  107.6 17.0 %mixer_forward.3 = (bf16[512,256]{1,0:T(8,128)(2,1)S(1)}, f32[512,1280]{1,0:T(8,128)}, f32[512,256]{1,0:T(8,128)}, f32[16,128,128]{2,1,0:T(8,128)}, f32[16,128,1...) custom-call(f32[1024,1664]{1,0:T(8,128)} %fusion.125.raw_ref, ...), custom_call_target="tpu_custom_call" | custom-call | tf_op jit(solution)/shard_map/mixer_forward/pallas_call | solution.py:447
  134.0 4.6 %collective-permute-done.7 = bf16[256,256]{1,0:T(8,128)(2,1)} collective-permute-done((bf16[256,256]{1,0:T(8,128)(2,1)}, bf16[256,256]{1,0:T(8,128)(2,1)}, u32[]{:S(2)}, u32[]{:S(2)}) %collective-permute-start.7) | collective-permute-done | bytes 131104 | tf_op jit(solution)/shard_map/ppermute | solution.py:591
  138.7 2.6 multiply_reduce_fusion.3
  142.5 2.7 collective-permute-start.8
  145.2 3.2 fusion.18
  148.4 3.1 multiply_convert_fusion.12
  157.7 2.7 multiply_convert_fusion.9
  163.4 3.2 fusion.10
  187.6 2.6 fusion.115
  192.5 2.5 collective-permute-start.11
  196.4 7.6 %collective-permute-done.11 = bf16[256,256]{1,0:T(8,128)(2,1)S(1)} collective-permute-done((bf16[256,256]{1,0:T(8,128)(2,1)S(1)}, bf16[256,256]{1,0:T(8,128)(2,1)S(1)}, u32[]{:S(2)}, u32[]{:S(2)}) %collective-permute-start.11) | collective-permute-done | bytes 131104 | tf_op jit(solution)/shard_map/ppermute | solution.py:591
  204.1 18.4 %mixer_backward.2 = (bf16[1024,1664]{1,0:T(8,128)(2,1)}, f32[4,1280]{1,0:T(4,128)S(1)}, f32[1,128]{1,0:T(1,128)S(1)}, f32[1,128]{1,0:T(1,128)S(1)}, f32[2,128,128]{2,1,0:T(8,128)S(1)}, /*index=5*/f32[8,1280]{1,0:T(8,128)S(1)}) custom-call(bf16[1024,256]{1,0:T(8,128)(2,1)S(1)} %constant_dynamic-update-slice_fusion.11.grad_ref, f32[1024,1664]{1,0:T(8,128)} %fusion.125.raw_ref, ...), custom_call_target="tpu_custom_call" | custom-call | tf_op jit(solution)/shard_map/mixer_backward/pallas_call | solution.py:518
  228.5 3.2 pad_maximum_fusion
  231.8 3.1 fusion.60
  234.9 2.9 reduce-scatter.3.cloned.1.call-done
  240.3 3.2 fusion.37
  246.8 19.6 %mixer_backward.3 = (bf16[1024,1664]{1,0:T(8,128)(2,1)}, f32[4,1280]{1,0:T(4,128)S(1)}, f32[1,128]{1,0:T(1,128)S(1)}, f32[1,128]{1,0:T(1,128)S(1)}, f32[2,128,128]{2,1,0:T(8,128)}, /*index=5*/f32[8,1280]{1,0:T(8,128)}) custom-call(bf16[1024,256]{1,0:T(8,128)(2,1)S(1)} %constant_dynamic-update-slice_fusion.11.grad_ref, ...), custom_call_target="tpu_custom_call", output_to_operand_aliasing={{0}: (19, {})} | custom-call | tf_op jit(solution)/shard_map/mixer_backward/pallas_call | solution.py:518
  266.4 2.4 collective-permute-done.13
  268.8 7.4 %convolution_convert_fusion.3 = bf16[1024,1024]{1,0:T(8,128)(2,1)} fusion(bf16[1024,1664]{1,0:T(8,128)(2,1)} %get-tuple-element.217, bf16[1024,1664]{1,0:T(8,128)(2,1)S(1)} %copy-done.63), kind=kOutput, calls=%fused_computation.30 | convolution fusion | flops 3490709504 | bytes 8912896 | tf_op jit(solution)/shard_map/dot_general | solution.py:586
  276.3 3.5 convolution_convert_fusion.2
  280.7 4.9 %all-to-all-start.1 = ((bf16[4,256,1024]{2,1,0:T(8,128)(2,1)}), bf16[4,256,1024]{2,1,0:T(8,128)(2,1)}, u32[]{:S(2)}, u32[]{:S(2)}) async-start(bf16[4,256,1024]{2,1,0:T(8,128)(2,1)} %bitcast.106), calls=%async_computation.3 | async-start | bytes 4194304 | tf_op jit(solution)/shard_map/all_to_all | solution.py:595
  285.8 5.1 %add_convert_fusion = bf16[512,1664]{1,0:T(8,128)(2,1)S(1)} fusion(bf16[512,1664]{1,0:T(8,128)(2,1)} %collective-permute-done.15, bf16[1024,1664]{1,0:T(8,128)(2,1)} %get-tuple-element.217, pred[]{:T(512)S(6)} %eq.61, bf16[1024,128]{1,0:T(8,128)(2,1)S(1)} %copy-done.36, bf16[1024,128]{1,0:T(8,128)(2,1)S(1)} %copy-done.38, ...), kind=kOutput, calls=%fused_computation.12 | convolution fusion | flops 1756299264 | bytes 8912897 | tf_op jit(solution)/shard_map/dot_general | solution.py:586
  298.7 3.0 add_convert_fusion.1
  301.7 12.0 %collective-permute-done.16 = bf16[128,1664]{1,0:T(8,128)(2,1)} collective-permute-done((bf16[128,1664]{1,0:T(8,128)(2,1)}, bf16[128,1664]{1,0:T(8,128)(2,1)}, u32[]{:S(2)}, u32[]{:S(2)}) %collective-permute-start.16) | collective-permute-done | bytes 426016 | tf_op jit(solution)/shard_map/ppermute | solution.py:591
  313.7 10.0 %collective-permute-done.18 = bf16[128,1664]{1,0:T(8,128)(2,1)} collective-permute-done((bf16[128,1664]{1,0:T(8,128)(2,1)}, bf16[128,1664]{1,0:T(8,128)(2,1)}, u32[]{:S(2)}, u32[]{:S(2)}) %collective-permute-start.18) | collective-permute-done | bytes 426016 | tf_op jit(solution)/shard_map/ppermute | solution.py:591
  334.5 3.3 collective-permute-done.20
  (346 shorter events, 110.4 us)
Async XLA Ops:
  7.3 69.3 %all-gather.5.cloned.1.call-start = ((), (), s32[]{:S(2)}) async-start(), calls=%async_computation.4 | async-start | bytes 3833856 | tf_op jit(solution)/shard_map/all_gather | solution.py:688
  11.2 78.0 %all-gather.7.cloned.1.call-start = ((), (), s32[]{:S(2)}) async-start(), calls=%async_computation.5 | async-start | bytes 5308416 | tf_op jit(solution)/shard_map/all_gather | solution.py:694
  12.2 54.7 %all-to-all-start = ((bf16[4,256,1024]{2,1,0:T(8,128)(2,1)}), bf16[4,256,1024]{2,1,0:T(8,128)(2,1)S(1)}, u32[]{:S(2)}, u32[]{:S(2)}) async-start(bf16[4,256,1024]{2,1,0:T(8,128)(2,1)} %broadcast_in_dim.18), calls=%async_computation | async-start | bytes 4194304 | tf_op jit(solution)/shard_map/all_to_all | solution.py:595
  18.7 113.8 %all-gather.9.cloned.1.call-start = ((), (), s32[]{:S(2)}) async-start(), calls=%async_computation.6 | async-start | bytes 2359296 | tf_op jit(solution)/shard_map/all_gather | solution.py:725
  66.9 7.4 %collective-permute-start = (bf16[128,256]{0,1:T(8,128)(2,1)S(1)}, bf16[128,256]{0,1:T(8,128)(2,1)S(1)}, u32[]{:S(2)}, u32[]{:S(2)}) collective-permute-start(bf16[128,256]{0,1:T(8,128)(2,1)S(1)} %bitcast.121), channel_id=1, source_target_pairs={{0,8},{8,0},{16,24},{24,16},{1,9},{9,1},{17,25},{25,17},{2,10},{10... | collective-permute-start | bytes 196616 | tf_op jit(solution)/shard_map/ppermute | solution.py:591
  66.9 7.4 %collective-permute-start.1 = (bf16[128,256]{0,1:T(8,128)(2,1)S(1)}, bf16[128,256]{0,1:T(8,128)(2,1)S(1)}, u32[]{:S(2)}, u32[]{:S(2)}) collective-permute-start(bf16[128,256]{0,1:T(8,128)(2,1)S(1)} %bitcast.122), channel_id=1, source_target_pairs={{0,16},{8,24},{16,0},{24,8},{1,17},{9,25},{17,1},{25,9},{2,18},{10... | collective-permute-start | bytes 196616 | tf_op jit(solution)/shard_map/ppermute | solution.py:591
  68.9 6.1 %collective-permute-start.2 = (bf16[128,256]{0,1:T(8,128)(2,1)S(1)}, bf16[128,256]{0,1:T(8,128)(2,1)S(1)}, u32[]{:S(2)}, u32[]{:S(2)}) collective-permute-start(bf16[128,256]{0,1:T(8,128)(2,1)S(1)} %bitcast.123), channel_id=1, source_target_pairs={{0,24},{8,16},{16,8},{24,0},{1,25},{9,17},{17,9},{25,1},{2,26},{10... | collective-permute-start | bytes 196616 | tf_op jit(solution)/shard_map/ppermute | solution.py:591
  75.8 87.6 %all-gather.11.cloned.1.call-start = ((), (), s32[]{:S(2)}) async-start(), calls=%async_computation.7 | async-start | bytes 5308416 | tf_op jit(solution)/shard_map/all_gather | solution.py:741
  76.2 29.5 %collective-permute-start.3 = (bf16[128,2304]{0,1:T(8,128)(2,1)}, bf16[128,2304]{0,1:T(8,128)(2,1)}, u32[]{:S(2)}, u32[]{:S(2)}) collective-permute-start(bf16[128,2304]{0,1:T(8,128)(2,1)} %fusion.90), channel_id=1, source_target_pairs={{0,16},{8,24},{16,0},{24,8},{1,17},{9,25},{17,1},{25,9},{2,18},{10... | collective-permute-start | bytes 1769480 | tf_op jit(solution)/shard_map/ppermute | solution.py:591
  105.8 132.1 %reduce-scatter.3.cloned.1.call-start = ((), (), s32[]{:S(2)}) async-start(), calls=%async_computation.8 | async-start | bytes 5308416 | tf_op jit(solution)/shard_map/reduce_scatter | solution.py:799
  106.0 18.5 %collective-permute-start.4 = (bf16[256,1024]{1,0:T(8,128)(2,1)}, bf16[256,1024]{1,0:T(8,128)(2,1)}, u32[]{:S(2)}, u32[]{:S(2)}) collective-permute-start(bf16[256,1024]{1,0:T(8,128)(2,1)} %param.20), channel_id=1, source_target_pairs={{0,8},{8,0},{16,24},{24,16},{1,9},{9,1},{17,25},{25,17},{2,10},{10... | collective-permute-start | bytes 1572872 | tf_op jit(solution)/shard_map/ppermute | solution.py:591
  125.4 8.4 %collective-permute-start.5 = (bf16[256,256]{1,0:T(8,128)(2,1)}, bf16[256,256]{1,0:T(8,128)(2,1)}, u32[]{:S(2)}, u32[]{:S(2)}) collective-permute-start(bf16[256,256]{1,0:T(8,128)(2,1)} %get-tuple-element.335), channel_id=1, source_target_pairs={{0,8},{8,0},{16,24},{24,16},{1,9},{9,1},{17,25},{25,17},{2,10},{10... | collective-permute-start | bytes 393224 | tf_op jit(solution)/shard_map/ppermute | solution.py:591
  125.9 8.1 %collective-permute-start.6 = (bf16[256,256]{1,0:T(8,128)(2,1)}, bf16[256,256]{1,0:T(8,128)(2,1)}, u32[]{:S(2)}, u32[]{:S(2)}) collective-permute-start(bf16[256,256]{1,0:T(8,128)(2,1)} %get-tuple-element.334), channel_id=1, source_target_pairs={{0,16},{8,24},{16,0},{24,8},{1,17},{9,25},{17,1},{25,9},{2,18},{10... | collective-permute-start | bytes 393224 | tf_op jit(solution)/shard_map/ppermute | solution.py:591
  128.4 10.3 %collective-permute-start.7 = (bf16[256,256]{1,0:T(8,128)(2,1)}, bf16[256,256]{1,0:T(8,128)(2,1)}, u32[]{:S(2)}, u32[]{:S(2)}) collective-permute-start(bf16[256,256]{1,0:T(8,128)(2,1)} %get-tuple-element.333), channel_id=1, source_target_pairs={{0,24},{8,16},{16,8},{24,0},{1,25},{9,17},{17,9},{25,1},{2,26},{10... | collective-permute-start | bytes 393224 | tf_op jit(solution)/shard_map/ppermute | solution.py:591
  142.5 14.2 %collective-permute-start.8 = (bf16[256,1024]{1,0:T(8,128)(2,1)S(1)}, bf16[256,1024]{1,0:T(8,128)(2,1)S(1)}, u32[]{:S(2)}, u32[]{:S(2)}) collective-permute-start(bf16[256,1024]{1,0:T(8,128)(2,1)S(1)} %multiply_convert_fusion), channel_id=1, source_target_pairs={{0,8},{8,0},{16,24},{24,16},{1,9},{9,1},{17,25},{25,17},{2,10},{10... | collective-permute-start | bytes 1572872 | tf_op jit(solution)/shard_map/ppermute | solution.py:591
  170.7 13.0 %collective-permute-start.9 = (bf16[256,1024]{1,0:T(8,128)(2,1)}, bf16[256,1024]{1,0:T(8,128)(2,1)}, u32[]{:S(2)}, u32[]{:S(2)}) collective-permute-start(bf16[256,1024]{1,0:T(8,128)(2,1)} %fusion.38), channel_id=1, source_target_pairs={{0,8},{8,0},{16,24},{24,16},{1,9},{9,1},{17,25},{25,17},{2,10},{10... | collective-permute-start | bytes 1572872 | tf_op jit(solution)/shard_map/ppermute | solution.py:591
  183.7 143.2 %reduce-scatter.5.cloned.1.call-start = ((), (), s32[]{:S(2)}) async-start(), calls=%async_computation.9 | async-start | bytes 7667712 | tf_op jit(solution)/shard_map/reduce_scatter | solution.py:817
  191.0 5.4 %collective-permute-start.10 = (bf16[256,256]{1,0:T(8,128)(2,1)S(1)}, bf16[256,256]{1,0:T(8,128)(2,1)S(1)}, u32[]{:S(2)}, u32[]{:S(2)}) collective-permute-start(bf16[256,256]{1,0:T(8,128)(2,1)S(1)} %get-tuple-element.330), channel_id=1, source_target_pairs={{0,8},{8,0},{16,24},{24,16},{1,9},{9,1},{17,25},{25,17},{2,10},{10... | collective-permute-start | bytes 393224 | tf_op jit(solution)/shard_map/ppermute | solution.py:591
  192.5 11.5 %collective-permute-start.11 = (bf16[256,256]{1,0:T(8,128)(2,1)S(1)}, bf16[256,256]{1,0:T(8,128)(2,1)S(1)}, u32[]{:S(2)}, u32[]{:S(2)}) collective-permute-start(bf16[256,256]{1,0:T(8,128)(2,1)S(1)} %get-tuple-element.329), channel_id=1, source_target_pairs={{0,16},{8,24},{16,0},{24,8},{1,17},{9,25},{17,1},{25,9},{2,18},{10... | collective-permute-start | bytes 393224 | tf_op jit(solution)/shard_map/ppermute | solution.py:591
  195.1 8.9 %collective-permute-start.12 = (bf16[256,256]{1,0:T(8,128)(2,1)S(1)}, bf16[256,256]{1,0:T(8,128)(2,1)S(1)}, u32[]{:S(2)}, u32[]{:S(2)}) collective-permute-start(bf16[256,256]{1,0:T(8,128)(2,1)S(1)} %get-tuple-element.328), channel_id=1, source_target_pairs={{0,24},{8,16},{16,8},{24,0},{1,25},{9,17},{17,9},{25,1},{2,26},{10... | collective-permute-start | bytes 393224 | tf_op jit(solution)/shard_map/ppermute | solution.py:591
  237.8 31.0 %collective-permute-start.14 = (bf16[128,2304]{1,0:T(8,128)(2,1)}, bf16[128,2304]{1,0:T(8,128)(2,1)}, u32[]{:S(2)}, u32[]{:S(2)}) collective-permute-start(bf16[128,2304]{1,0:T(8,128)(2,1)} %reduce-scatter.3.cloned.1.call-done), channel_id=1, source_target_pairs={{0,16},{8,24},{16,0},{24,8},{1,17},{9,25},{17,1},{25,9},{2,18},{10... | collective-permute-start | bytes 1769480 | tf_op jit(solution)/shard_map/ppermute | solution.py:591
  243.5 25.3 %collective-permute-start.13 = (bf16[256,1024]{1,0:T(8,128)(2,1)}, bf16[256,1024]{1,0:T(8,128)(2,1)}, u32[]{:S(2)}, u32[]{:S(2)}) collective-permute-start(bf16[256,1024]{1,0:T(8,128)(2,1)} %fusion.37), channel_id=1, source_target_pairs={{0,8},{8,0},{16,24},{24,16},{1,9},{9,1},{17,25},{25,17},{2,10},{10... | collective-permute-start | bytes 1572872 | tf_op jit(solution)/shard_map/ppermute | solution.py:591
  279.8 6.0 %collective-permute-start.15 = (bf16[512,1664]{1,0:T(8,128)(2,1)}, bf16[512,1664]{1,0:T(8,128)(2,1)}, u32[]{:S(2)}, u32[]{:S(2)}) collective-permute-start(bf16[512,1664]{1,0:T(8,128)(2,1)} %convolution_convert_fusion.2), channel_id=1, source_target_pairs={{0,1},{1,0},{2,3},{3,2},{4,5},{5,4},{6,7},{7,6},{8,9},{9,8},{10,11... | collective-permute-start | bytes 5111816 | tf_op jit(solution)/shard_map/ppermute | solution.py:591
  280.7 61.4 %all-to-all-start.1 = ((bf16[4,256,1024]{2,1,0:T(8,128)(2,1)}), bf16[4,256,1024]{2,1,0:T(8,128)(2,1)}, u32[]{:S(2)}, u32[]{:S(2)}) async-start(bf16[4,256,1024]{2,1,0:T(8,128)(2,1)} %bitcast.106), calls=%async_computation.3 | async-start | bytes 4194304 | tf_op jit(solution)/shard_map/all_to_all | solution.py:595
  292.0 21.6 %collective-permute-start.16 = (bf16[128,1664]{1,0:T(8,128)(2,1)}, bf16[128,1664]{1,0:T(8,128)(2,1)}, u32[]{:S(2)}, u32[]{:S(2)}) collective-permute-start(bf16[128,1664]{1,0:T(8,128)(2,1)} %get-tuple-element.314), channel_id=1, source_target_pairs={{0,2},{1,3},{2,0},{3,1},{4,6},{5,7},{6,4},{7,5},{8,10},{9,11},{10,... | collective-permute-start | bytes 1277960 | tf_op jit(solution)/shard_map/ppermute | solution.py:591
  293.5 20.2 %collective-permute-start.17 = (bf16[128,1664]{1,0:T(8,128)(2,1)}, bf16[128,1664]{1,0:T(8,128)(2,1)}, u32[]{:S(2)}, u32[]{:S(2)}) collective-permute-start(bf16[128,1664]{1,0:T(8,128)(2,1)} %get-tuple-element.316), channel_id=1, source_target_pairs={{0,4},{1,5},{2,6},{3,7},{4,0},{5,1},{6,2},{7,3},{8,12},{9,13},{10,... | collective-permute-start | bytes 1277960 | tf_op jit(solution)/shard_map/ppermute | solution.py:591
  294.1 29.6 %collective-permute-start.18 = (bf16[128,1664]{1,0:T(8,128)(2,1)}, bf16[128,1664]{1,0:T(8,128)(2,1)}, u32[]{:S(2)}, u32[]{:S(2)}) collective-permute-start(bf16[128,1664]{1,0:T(8,128)(2,1)} %get-tuple-element.315), channel_id=1, source_target_pairs={{0,6},{1,7},{2,4},{3,5},{4,2},{5,3},{6,0},{7,1},{8,14},{9,15},{10,... | collective-permute-start | bytes 1277960 | tf_op jit(solution)/shard_map/ppermute | solution.py:591
  327.9 10.4 %collective-permute-start.24 = (bf16[128,256]{1,0:T(8,128)(2,1)S(1)}, bf16[128,256]{1,0:T(8,128)(2,1)S(1)}, u32[]{:S(2)}, u32[]{:S(2)}) collective-permute-start(bf16[128,256]{1,0:T(8,128)(2,1)S(1)} %get-tuple-element.336), channel_id=1, source_target_pairs={{0,8},{8,0},{16,24},{24,16},{1,9},{9,1},{17,25},{25,17},{2,10},{10... | collective-permute-start | bytes 196616 | tf_op jit(solution)/shard_map/ppermute | solution.py:591
  329.5 9.9 %collective-permute-start.25 = (bf16[128,256]{1,0:T(8,128)(2,1)S(1)}, bf16[128,256]{1,0:T(8,128)(2,1)S(1)}, u32[]{:S(2)}, u32[]{:S(2)}) collective-permute-start(bf16[128,256]{1,0:T(8,128)(2,1)S(1)} %get-tuple-element.338), channel_id=1, source_target_pairs={{0,16},{8,24},{16,0},{24,8},{1,17},{9,25},{17,1},{25,9},{2,18},{10... | collective-permute-start | bytes 196616 | tf_op jit(solution)/shard_map/ppermute | solution.py:591
  331.9 7.5 %collective-permute-start.26 = (bf16[128,256]{1,0:T(8,128)(2,1)S(1)}, bf16[128,256]{1,0:T(8,128)(2,1)S(1)}, u32[]{:S(2)}, u32[]{:S(2)}) collective-permute-start(bf16[128,256]{1,0:T(8,128)(2,1)S(1)} %get-tuple-element.337), channel_id=1, source_target_pairs={{0,24},{8,16},{16,8},{24,0},{1,25},{9,17},{17,9},{25,1},{2,26},{10... | collective-permute-start | bytes 196616 | tf_op jit(solution)/shard_map/ppermute | solution.py:591
  342.1 4.6 %collective-permute-start.22 = (f32[184,128]{1,0:T(8,128)S(1)}, f32[184,128]{1,0:T(8,128)S(1)}, u32[]{:S(2)}, u32[]{:S(2)}) collective-permute-start(f32[184,128]{1,0:T(8,128)S(1)} %pad_bitcast_fusion), channel_id=1, source_target_pairs={{0,8},{8,0},{16,24},{24,16},{1,9},{9,1},{17,25},{25,17},{2,10},{10... | collective-permute-start | bytes 282632 | tf_op jit(solution)/shard_map/ppermute | solution.py:591
  346.8 6.6 %collective-permute-start.23 = (f32[184,128]{1,0:T(8,128)S(1)}, f32[184,128]{1,0:T(8,128)S(1)}, u32[]{:S(2)}, u32[]{:S(2)}) collective-permute-start(f32[184,128]{1,0:T(8,128)S(1)} %add.244), channel_id=1, source_target_pairs={{0,16},{8,24},{16,0},{24,8},{1,17},{9,25},{17,1},{25,9},{2,18},{10... | collective-permute-start | bytes 282632 | tf_op jit(solution)/shard_map/ppermute | solution.py:591
  (74 other events, 688.6 us)
Sparse Core Ops, SparseCore 0:
  11.3 36.1 all-gather.4
  49.4 39.7 all-gather.6
  91.6 28.1 all-gather.8
  121.6 39.7 all-gather.10
  183.8 53.9 reduce-scatter.2
  241.5 73.3 reduce-scatter.4
where the time goes:
time: 368 us; the launch traced here: 364 us
  waiting for transfers between devices  102 us (28%)
  matrix products  75.3 us (20%)
  Pallas kernels  71.5 us (19%)
  starting transfers between devices  47.7 us (13%)
  local copies, waits for them, and re-layouts  26.2 us (7%)
  other arithmetic  26.2 us (7%)
  between operations  15.7 us (4%)
    dot_general x27, matrix products, dot(): lax.dot_general(left, right, (dims, ((), ())), preferred_element_type=jnp...  75.3 us
    ppermute x27, waiting for transfers between devices, swap(): return lax.ppermute(x, axis, [(i, i ^ bit) for i in range(size)])  49.3 us
    all_to_all x2, waiting for transfers between devices, exchange(): return lax.all_to_all(blocks, axis, split_axis=0, concat_axis=0, tiled=True)  46 us
    pallas_call x2, Pallas kernels, mixer_backward(): pl.pallas_call(partial(bwd_kernel, heads, per_step), grid=(steps,), in_sp...  38 us
    ppermute x27, starting transfers between devices, swap(): return lax.ppermute(x, axis, [(i, i ^ bit) for i in range(size)])  35.8 us
    pallas_call x2, Pallas kernels, mixer_forward(): pl.pallas_call(partial(fwd_kernel, heads, per_step), grid=(steps,), in_sp...  33.5 us
    all_to_all x2, starting transfers between devices, exchange(): return lax.all_to_all(blocks, axis, split_axis=0, concat_axis=0, tiled=True)  11.3 us
    unnamed x163, local copies, waits for them, and re-layouts  8.65 us
  transfers between devices with their start and end apart: 35, of which 18 were waited for; matrix products, arithmetic and copies ran while one was open for 30% of the time, Pallas kernels for 20%

commit v1 on v0

--- a/solution.py
+++ b/solution.py
@@ -800,7 +800,8 @@
     ]
     downs = [ff_set[:, 2 * ff_pad : 3 * ff_pad] for ff_set in ff_sets]
     out_pair = sum(dot(hidden, down, NT) for hidden, down in zip(out_hidden, downs))
-    out_swap = swap(out_pair.astype(bf16), "head", 1)
+    out_pair, mixed_grad = lax.optimization_barrier((out_pair.astype(bf16), mixed_grad))
+    out_swap = swap(out_pair, "head", 1)
 
     carry = None
     for part in reversed(range(SPANS)):

time: 368 us -> 377 us (1.024)
  matrix products: 75.3 us -> 85.3 us
    dot_general x27, matrix products: 75.3 us -> 85.3 us  [dot(): lax.dot_general(left, right, (dims, ((), ())), preferred_element_type=jnp...]
    ppermute x27, waiting for transfers between devices: 49.3 us -> 54 us  [swap(): return lax.ppermute(x, axis, [(i, i ^ bit) for i in range(size)])]
    unnamed x163 -> x165, local copies, waits for them, and re-layouts: 8.65 us -> 8.67 us
  transfers between devices with their start and end apart: 35 -> 35, of which waited for: 18 -> 17; matrix products, arithmetic and copies ran while one was open for 30% -> 32% of each run, Pallas kernels for 20% -> 19%
where the time goes in v1:
time: 377 us; the launch traced here: 374 us
  waiting for transfers between devices  103 us (27%)
  matrix products  85.3 us (23%)
  Pallas kernels  70.7 us (19%)
  starting transfers between devices  46 us (12%)
  other arithmetic  26.4 us (7%)
  local copies, waits for them, and re-layouts  26.2 us (7%)
  between operations  15.6 us (4%)
    dot_general x27, matrix products, dot(): lax.dot_general(left, right, (dims, ((), ())), preferred_element_type=jnp...  85.3 us
    ppermute x27, waiting for transfers between devices, swap(): return lax.ppermute(x, axis, [(i, i ^ bit) for i in range(size)])  54 us
    all_to_all x2, waiting for transfers between devices, exchange(): return lax.all_to_all(blocks, axis, split_axis=0, concat_axis=0, tiled=True)  46 us
    pallas_call x2, Pallas kernels, mixer_backward(): pl.pallas_call(partial(bwd_kernel, heads, per_step), grid=(steps,), in_sp...  37.3 us
    ppermute x27, starting transfers between devices, swap(): return lax.ppermute(x, axis, [(i, i ^ bit) for i in range(size)])  34.2 us
    pallas_call x2, Pallas kernels, mixer_forward(): pl.pallas_call(partial(fwd_kernel, heads, per_step), grid=(steps,), in_sp...  33.4 us
    all_to_all x2, starting transfers between devices, exchange(): return lax.all_to_all(blocks, axis, split_axis=0, concat_axis=0, tiled=True)  11.2 us
    unnamed x165, local copies, waits for them, and re-layouts  8.67 us
  transfers between devices with their start and end apart: 35, of which 17 were waited for; matrix products, arithmetic and copies ran while one was open for 32% of the time, Pallas kernels for 19%

profile of v1, /device:TPU:0, one launch (start us, length us, event | category | flops | bytes accessed | tf_op | source)
XLA Modules:
  0.0 373.8 jit_solution(14909042626686143668)
XLA Ops:
  7.3 2.8 broadcast_in_dim.17
  12.2 6.5 %all-to-all-start = ((bf16[4,256,1024]{2,1,0:T(8,128)(2,1)}), bf16[4,256,1024]{2,1,0:T(8,128)(2,1)S(1)}, u32[]{:S(2)}, u32[]{:S(2)}) async-start(bf16[4,256,1024]{2,1,0:T(8,128)(2,1)} %broadcast_in_dim.17), calls=%async_computation | async-start | bytes 4194304 | tf_op jit(solution)/shard_map/all_to_all | solution.py:595
  20.9 46.0 %all-to-all-done = bf16[4,256,1024]{2,1,0:T(8,128)(2,1)S(1)} async-done(((bf16[4,256,1024]{2,1,0:T(8,128)(2,1)}), bf16[4,256,1024]{2,1,0:T(8,128)(2,1)S(1)}, u32[]{:S(2)}, u32[]{:S(2)}) %all-to-all-start) | async-done | bytes 2097184 | tf_op jit(solution)/shard_map/all_to_all | solution.py:595
  76.6 9.4 %fusion.125.raw_ref = f32[1024,1664]{1,0:T(8,128)} fusion(bf16[1024,1024]{1,0:T(8,128)(2,1)} %fusion.3, bf16[1024,1664]{1,0:T(8,128)(2,1)} %all-gather.5.cloned.1.call-done), kind=kOutput, calls=%fused_computation.231 | convolution fusion | flops 3489660928 | bytes 12320768 | tf_op jit(solution)/shard_map/dot_general | solution.py:586
  86.1 3.1 all-gather.7.cloned.1.call-done
  89.2 16.5 %mixer_forward.2 = (bf16[512,256]{1,0:T(8,128)(2,1)S(1)}, f32[512,1280]{1,0:T(8,128)}, f32[512,256]{1,0:T(8,128)}, f32[16,128,128]{2,1,0:T(8,128)}, f32[16,128,1...) custom-call(f32[1024,1664]{1,0:T(8,128)} %fusion.125.raw_ref, ...), custom_call_target="tpu_custom_call" | custom-call | tf_op jit(solution)/shard_map/mixer_forward/pallas_call | solution.py:447
  107.6 16.9 %mixer_forward.3 = (bf16[512,256]{1,0:T(8,128)(2,1)S(1)}, f32[512,1280]{1,0:T(8,128)}, f32[512,256]{1,0:T(8,128)}, f32[16,128,128]{2,1,0:T(8,128)}, f32[16,128,1...) custom-call(f32[1024,1664]{1,0:T(8,128)} %fusion.125.raw_ref, ...), custom_call_target="tpu_custom_call" | custom-call | tf_op jit(solution)/shard_map/mixer_forward/pallas_call | solution.py:447
  133.9 6.2 %collective-permute-done.6 = bf16[256,256]{1,0:T(8,128)(2,1)} collective-permute-done((bf16[256,256]{1,0:T(8,128)(2,1)}, bf16[256,256]{1,0:T(8,128)(2,1)}, u32[]{:S(2)}, u32[]{:S(2)}) %collective-permute-start.6) | collective-permute-done | bytes 131104 | tf_op jit(solution)/shard_map/ppermute | solution.py:591
  140.1 2.6 multiply_reduce_fusion.3
  144.0 3.3 fusion.18
  147.3 3.1 multiply_convert_fusion.12
  153.4 3.9 %collective-permute-done.8 = bf16[256,1024]{1,0:T(8,128)(2,1)S(1)} collective-permute-done((bf16[256,1024]{1,0:T(8,128)(2,1)S(1)}, bf16[256,1024]{1,0:T(8,128)(2,1)S(1)}, u32[]{:S(2)}, u32[]{:S(2)}) %collective-permute-start.8) | collective-permute-done | bytes 524320 | tf_op jit(solution)/shard_map/ppermute | solution.py:591
  158.3 2.7 multiply_convert_fusion.9
  163.8 3.2 fusion.10
  173.5 13.4 %convolution_convert_fusion.1 = bf16[1024,1536]{1,0:T(8,128)(2,1)S(1)} fusion(bf16[256,768]{1,0:T(8,128)(2,1)S(1)} %get-tuple-element.305, bf16[256,768]{1,0:T(8,128)(2,1)S(1)} %get-tuple-element.304, bf16[256,768]{1,0:T(8,128)(2,1)S(1)} %get-tuple-element.303, bf16[256,768]{1,0:T(8,128)(2,1)S(1)} %get-tuple-element.302, ...), kind=kOutput, calls=%fused_computation.11 | convolution fusion | flops 1620574208 | bytes 5767168 | tf_op jit(solution)/shard_map/dot_general | solution.py:586
  197.5 2.7 fusion.115
  207.2 7.0 %collective-permute-done.11 = bf16[256,256]{1,0:T(8,128)(2,1)S(1)} collective-permute-done((bf16[256,256]{1,0:T(8,128)(2,1)S(1)}, bf16[256,256]{1,0:T(8,128)(2,1)S(1)}, u32[]{:S(2)}, u32[]{:S(2)}) %collective-permute-start.11) | collective-permute-done | bytes 131104 | tf_op jit(solution)/shard_map/ppermute | solution.py:591
  216.2 2.9 fusion.37
  219.1 18.3 %mixer_backward.2 = (bf16[1024,1664]{1,0:T(8,128)(2,1)}, f32[4,1280]{1,0:T(4,128)S(1)}, f32[1,128]{1,0:T(1,128)S(1)}, f32[1,128]{1,0:T(1,128)S(1)}, f32[2,128,128]{2,1,0:T(8,128)S(1)}, /*index=5*/f32[8,1280]{1,0:T(8,128)S(1)}) custom-call(bf16[1024,256]{1,0:T(8,128)(2,1)S(1)} %constant_dynamic-update-slice_fusion.11.grad_ref, f32[1024,1664]{1,0:T(8,128)} %fusion.125.raw_ref, ...), custom_call_target="tpu_custom_call" | custom-call | tf_op jit(solution)/shard_map/mixer_backward/pallas_call | solution.py:518
  243.5 3.2 pad_maximum_fusion
  247.0 2.9 collective-permute-start.14
  252.7 19.0 %mixer_backward.3 = (bf16[1024,1664]{1,0:T(8,128)(2,1)}, f32[4,1280]{1,0:T(4,128)S(1)}, f32[1,128]{1,0:T(1,128)S(1)}, f32[1,128]{1,0:T(1,128)S(1)}, f32[2,128,128]{2,1,0:T(8,128)}, /*index=5*/f32[8,1280]{1,0:T(8,128)}) custom-call(bf16[1024,256]{1,0:T(8,128)(2,1)S(1)} %constant_dynamic-update-slice_fusion.11.grad_ref, ...), custom_call_target="tpu_custom_call", output_to_operand_aliasing={{0}: (19, {})} | custom-call | tf_op jit(solution)/shard_map/mixer_backward/pallas_call | solution.py:518
  275.9 7.5 %convolution_convert_fusion.3 = bf16[1024,1024]{1,0:T(8,128)(2,1)} fusion(bf16[1024,1664]{1,0:T(8,128)(2,1)} %get-tuple-element.221, bf16[1024,1664]{1,0:T(8,128)(2,1)S(1)} %copy-done.64), kind=kOutput, calls=%fused_computation.30 | convolution fusion | flops 3490709504 | bytes 8912896 | tf_op jit(solution)/shard_map/dot_general | solution.py:586
  283.5 3.4 convolution_convert_fusion.2
  287.9 4.8 %all-to-all-start.1 = ((bf16[4,256,1024]{2,1,0:T(8,128)(2,1)}), bf16[4,256,1024]{2,1,0:T(8,128)(2,1)}, u32[]{:S(2)}, u32[]{:S(2)}) async-start(bf16[4,256,1024]{2,1,0:T(8,128)(2,1)} %bitcast.106), calls=%async_computation.3 | async-start | bytes 4194304 | tf_op jit(solution)/shard_map/all_to_all | solution.py:595
  292.9 4.9 %add_convert_fusion = bf16[512,1664]{1,0:T(8,128)(2,1)S(1)} fusion(bf16[512,1664]{1,0:T(8,128)(2,1)} %collective-permute-done.15, bf16[1024,1664]{1,0:T(8,128)(2,1)} %get-tuple-element.221, pred[]{:T(512)S(6)} %eq.61, bf16[1024,128]{1,0:T(8,128)(2,1)S(1)} %copy-done.37, bf16[1024,128]{1,0:T(8,128)(2,1)S(1)} %copy-done.39, ...), kind=kOutput, calls=%fused_computation.12 | convolution fusion | flops 1756299264 | bytes 8912897 | tf_op jit(solution)/shard_map/dot_general | solution.py:586
  305.5 3.0 add_convert_fusion.1
  308.5 12.0 %collective-permute-done.18 = bf16[128,1664]{1,0:T(8,128)(2,1)} collective-permute-done((bf16[128,1664]{1,0:T(8,128)(2,1)}, bf16[128,1664]{1,0:T(8,128)(2,1)}, u32[]{:S(2)}, u32[]{:S(2)}) %collective-permute-start.18) | collective-permute-done | bytes 426016 | tf_op jit(solution)/shard_map/ppermute | solution.py:591
  320.5 9.9 %collective-permute-done.17 = bf16[128,1664]{1,0:T(8,128)(2,1)} collective-permute-done((bf16[128,1664]{1,0:T(8,128)(2,1)}, bf16[128,1664]{1,0:T(8,128)(2,1)}, u32[]{:S(2)}, u32[]{:S(2)}) %collective-permute-start.17) | collective-permute-done | bytes 426016 | tf_op jit(solution)/shard_map/ppermute | solution.py:591
  336.2 3.6 collective-permute-start.26
  352.8 3.1 collective-permute-done.22
  355.8 2.5 collective-permute-start.23
  (348 shorter events, 107.9 us)
Async XLA Ops:
  7.3 69.3 %all-gather.5.cloned.1.call-start = ((), (), s32[]{:S(2)}) async-start(), calls=%async_computation.4 | async-start | bytes 3833856 | tf_op jit(solution)/shard_map/all_gather | solution.py:688
  11.2 78.0 %all-gather.7.cloned.1.call-start = ((), (), s32[]{:S(2)}) async-start(), calls=%async_computation.5 | async-start | bytes 5308416 | tf_op jit(solution)/shard_map/all_gather | solution.py:694
  12.2 54.7 %all-to-all-start = ((bf16[4,256,1024]{2,1,0:T(8,128)(2,1)}), bf16[4,256,1024]{2,1,0:T(8,128)(2,1)S(1)}, u32[]{:S(2)}, u32[]{:S(2)}) async-start(bf16[4,256,1024]{2,1,0:T(8,128)(2,1)} %broadcast_in_dim.17), calls=%async_computation | async-start | bytes 4194304 | tf_op jit(solution)/shard_map/all_to_all | solution.py:595
  18.7 113.8 %all-gather.9.cloned.1.call-start = ((), (), s32[]{:S(2)}) async-start(), calls=%async_computation.6 | async-start | bytes 2359296 | tf_op jit(solution)/shard_map/all_gather | solution.py:725
  66.9 7.4 %collective-permute-start = (bf16[128,256]{0,1:T(8,128)(2,1)S(1)}, bf16[128,256]{0,1:T(8,128)(2,1)S(1)}, u32[]{:S(2)}, u32[]{:S(2)}) collective-permute-start(bf16[128,256]{0,1:T(8,128)(2,1)S(1)} %bitcast.121), channel_id=1, source_target_pairs={{0,8},{8,0},{16,24},{24,16},{1,9},{9,1},{17,25},{25,17},{2,10},{10... | collective-permute-start | bytes 196616 | tf_op jit(solution)/shard_map/ppermute | solution.py:591
  66.9 7.4 %collective-permute-start.1 = (bf16[128,256]{0,1:T(8,128)(2,1)S(1)}, bf16[128,256]{0,1:T(8,128)(2,1)S(1)}, u32[]{:S(2)}, u32[]{:S(2)}) collective-permute-start(bf16[128,256]{0,1:T(8,128)(2,1)S(1)} %bitcast.122), channel_id=1, source_target_pairs={{0,16},{8,24},{16,0},{24,8},{1,17},{9,25},{17,1},{25,9},{2,18},{10... | collective-permute-start | bytes 196616 | tf_op jit(solution)/shard_map/ppermute | solution.py:591
  68.9 6.1 %collective-permute-start.2 = (bf16[128,256]{0,1:T(8,128)(2,1)S(1)}, bf16[128,256]{0,1:T(8,128)(2,1)S(1)}, u32[]{:S(2)}, u32[]{:S(2)}) collective-permute-start(bf16[128,256]{0,1:T(8,128)(2,1)S(1)} %bitcast.123), channel_id=1, source_target_pairs={{0,24},{8,16},{16,8},{24,0},{1,25},{9,17},{17,9},{25,1},{2,26},{10... | collective-permute-start | bytes 196616 | tf_op jit(solution)/shard_map/ppermute | solution.py:591
  75.8 88.0 %all-gather.11.cloned.1.call-start = ((), (), s32[]{:S(2)}) async-start(), calls=%async_computation.7 | async-start | bytes 5308416 | tf_op jit(solution)/shard_map/all_gather | solution.py:741
  76.2 29.5 %collective-permute-start.3 = (bf16[128,2304]{0,1:T(8,128)(2,1)}, bf16[128,2304]{0,1:T(8,128)(2,1)}, u32[]{:S(2)}, u32[]{:S(2)}) collective-permute-start(bf16[128,2304]{0,1:T(8,128)(2,1)} %fusion.90), channel_id=1, source_target_pairs={{0,16},{8,24},{16,0},{24,8},{1,17},{9,25},{17,1},{25,9},{2,18},{10... | collective-permute-start | bytes 1769480 | tf_op jit(solution)/shard_map/ppermute | solution.py:591
  105.8 141.2 %reduce-scatter.3.cloned.1.call-start = ((), (), s32[]{:S(2)}) async-start(), calls=%async_computation.8 | async-start | bytes 5308416 | tf_op jit(solution)/shard_map/reduce_scatter | solution.py:799
  106.0 18.4 %collective-permute-start.4 = (bf16[256,1024]{1,0:T(8,128)(2,1)}, bf16[256,1024]{1,0:T(8,128)(2,1)}, u32[]{:S(2)}, u32[]{:S(2)}) collective-permute-start(bf16[256,1024]{1,0:T(8,128)(2,1)} %param.20), channel_id=1, source_target_pairs={{0,8},{8,0},{16,24},{24,16},{1,9},{9,1},{17,25},{25,17},{2,10},{10... | collective-permute-start | bytes 1572872 | tf_op jit(solution)/shard_map/ppermute | solution.py:591
  125.3 8.6 %collective-permute-start.7 = (bf16[256,256]{1,0:T(8,128)(2,1)}, bf16[256,256]{1,0:T(8,128)(2,1)}, u32[]{:S(2)}, u32[]{:S(2)}) collective-permute-start(bf16[256,256]{1,0:T(8,128)(2,1)} %get-tuple-element.337), channel_id=1, source_target_pairs={{0,24},{8,16},{16,8},{24,0},{1,25},{9,17},{17,9},{25,1},{2,26},{10... | collective-permute-start | bytes 393224 | tf_op jit(solution)/shard_map/ppermute | solution.py:591
  127.7 12.4 %collective-permute-start.6 = (bf16[256,256]{1,0:T(8,128)(2,1)}, bf16[256,256]{1,0:T(8,128)(2,1)}, u32[]{:S(2)}, u32[]{:S(2)}) collective-permute-start(bf16[256,256]{1,0:T(8,128)(2,1)} %get-tuple-element.338), channel_id=1, source_target_pairs={{0,16},{8,24},{16,0},{24,8},{1,17},{9,25},{17,1},{25,9},{2,18},{10... | collective-permute-start | bytes 393224 | tf_op jit(solution)/shard_map/ppermute | solution.py:591
  127.7 12.4 %collective-permute-start.5 = (bf16[256,256]{1,0:T(8,128)(2,1)}, bf16[256,256]{1,0:T(8,128)(2,1)}, u32[]{:S(2)}, u32[]{:S(2)}) collective-permute-start(bf16[256,256]{1,0:T(8,128)(2,1)} %get-tuple-element.339), channel_id=1, source_target_pairs={{0,8},{8,0},{16,24},{24,16},{1,9},{9,1},{17,25},{25,17},{2,10},{10... | collective-permute-start | bytes 393224 | tf_op jit(solution)/shard_map/ppermute | solution.py:591
  143.9 13.3 %collective-permute-start.8 = (bf16[256,1024]{1,0:T(8,128)(2,1)S(1)}, bf16[256,1024]{1,0:T(8,128)(2,1)S(1)}, u32[]{:S(2)}, u32[]{:S(2)}) collective-permute-start(bf16[256,1024]{1,0:T(8,128)(2,1)S(1)} %multiply_convert_fusion), channel_id=1, source_target_pairs={{0,8},{8,0},{16,24},{24,16},{1,9},{9,1},{17,25},{25,17},{2,10},{10... | collective-permute-start | bytes 1572872 | tf_op jit(solution)/shard_map/ppermute | solution.py:591
  171.1 22.5 %collective-permute-start.9 = (bf16[256,1024]{1,0:T(8,128)(2,1)}, bf16[256,1024]{1,0:T(8,128)(2,1)}, u32[]{:S(2)}, u32[]{:S(2)}) collective-permute-start(bf16[256,1024]{1,0:T(8,128)(2,1)} %fusion.38), channel_id=1, source_target_pairs={{0,8},{8,0},{16,24},{24,16},{1,9},{9,1},{17,25},{25,17},{2,10},{10... | collective-permute-start | bytes 1572872 | tf_op jit(solution)/shard_map/ppermute | solution.py:591
  193.6 140.1 %reduce-scatter.5.cloned.1.call-start = ((), (), s32[]{:S(2)}) async-start(), calls=%async_computation.9 | async-start | bytes 7667712 | tf_op jit(solution)/shard_map/reduce_scatter | solution.py:818
  201.1 6.0 %collective-permute-start.10 = (bf16[256,256]{1,0:T(8,128)(2,1)S(1)}, bf16[256,256]{1,0:T(8,128)(2,1)S(1)}, u32[]{:S(2)}, u32[]{:S(2)}) collective-permute-start(bf16[256,256]{1,0:T(8,128)(2,1)S(1)} %get-tuple-element.335), channel_id=1, source_target_pairs={{0,8},{8,0},{16,24},{24,16},{1,9},{9,1},{17,25},{25,17},{2,10},{10... | collective-permute-start | bytes 393224 | tf_op jit(solution)/shard_map/ppermute | solution.py:591
  202.9 11.2 %collective-permute-start.11 = (bf16[256,256]{1,0:T(8,128)(2,1)S(1)}, bf16[256,256]{1,0:T(8,128)(2,1)S(1)}, u32[]{:S(2)}, u32[]{:S(2)}) collective-permute-start(bf16[256,256]{1,0:T(8,128)(2,1)S(1)} %get-tuple-element.333), channel_id=1, source_target_pairs={{0,16},{8,24},{16,0},{24,8},{1,17},{9,25},{17,1},{25,9},{2,18},{10... | collective-permute-start | bytes 393224 | tf_op jit(solution)/shard_map/ppermute | solution.py:591
  204.0 10.2 %collective-permute-start.12 = (bf16[256,256]{1,0:T(8,128)(2,1)S(1)}, bf16[256,256]{1,0:T(8,128)(2,1)S(1)}, u32[]{:S(2)}, u32[]{:S(2)}) collective-permute-start(bf16[256,256]{1,0:T(8,128)(2,1)S(1)} %get-tuple-element.332), channel_id=1, source_target_pairs={{0,24},{8,16},{16,8},{24,0},{1,25},{9,17},{17,9},{25,1},{2,26},{10... | collective-permute-start | bytes 393224 | tf_op jit(solution)/shard_map/ppermute | solution.py:591
  247.0 28.9 %collective-permute-start.14 = (bf16[128,2304]{1,0:T(8,128)(2,1)}, bf16[128,2304]{1,0:T(8,128)(2,1)}, u32[]{:S(2)}, u32[]{:S(2)}) collective-permute-start(bf16[128,2304]{1,0:T(8,128)(2,1)} %reduce-scatter.3.cloned.1.call-done), channel_id=1, source_target_pairs={{0,16},{8,24},{16,0},{24,8},{1,17},{9,25},{17,1},{25,9},{2,18},{10... | collective-permute-start | bytes 1769480 | tf_op jit(solution)/shard_map/ppermute | solution.py:591
  249.8 23.8 %collective-permute-start.13 = (bf16[256,1024]{1,0:T(8,128)(2,1)}, bf16[256,1024]{1,0:T(8,128)(2,1)}, u32[]{:S(2)}, u32[]{:S(2)}) collective-permute-start(bf16[256,1024]{1,0:T(8,128)(2,1)} %fusion.37), channel_id=1, source_target_pairs={{0,8},{8,0},{16,24},{24,16},{1,9},{9,1},{17,25},{25,17},{2,10},{10... | collective-permute-start | bytes 1572872 | tf_op jit(solution)/shard_map/ppermute | solution.py:591
  286.9 5.9 %collective-permute-start.15 = (bf16[512,1664]{1,0:T(8,128)(2,1)}, bf16[512,1664]{1,0:T(8,128)(2,1)}, u32[]{:S(2)}, u32[]{:S(2)}) collective-permute-start(bf16[512,1664]{1,0:T(8,128)(2,1)} %convolution_convert_fusion.2), channel_id=1, source_target_pairs={{0,1},{1,0},{2,3},{3,2},{4,5},{5,4},{6,7},{7,6},{8,9},{9,8},{10,11... | collective-permute-start | bytes 5111816 | tf_op jit(solution)/shard_map/ppermute | solution.py:591
  287.9 61.1 %all-to-all-start.1 = ((bf16[4,256,1024]{2,1,0:T(8,128)(2,1)}), bf16[4,256,1024]{2,1,0:T(8,128)(2,1)}, u32[]{:S(2)}, u32[]{:S(2)}) async-start(bf16[4,256,1024]{2,1,0:T(8,128)(2,1)} %bitcast.106), calls=%async_computation.3 | async-start | bytes 4194304 | tf_op jit(solution)/shard_map/all_to_all | solution.py:595
  298.9 21.6 %collective-permute-start.18 = (bf16[128,1664]{1,0:T(8,128)(2,1)}, bf16[128,1664]{1,0:T(8,128)(2,1)}, u32[]{:S(2)}, u32[]{:S(2)}) collective-permute-start(bf16[128,1664]{1,0:T(8,128)(2,1)} %get-tuple-element.319), channel_id=1, source_target_pairs={{0,6},{1,7},{2,4},{3,5},{4,2},{5,3},{6,0},{7,1},{8,14},{9,15},{10,... | collective-permute-start | bytes 1277960 | tf_op jit(solution)/shard_map/ppermute | solution.py:591
  301.0 29.5 %collective-permute-start.17 = (bf16[128,1664]{1,0:T(8,128)(2,1)}, bf16[128,1664]{1,0:T(8,128)(2,1)}, u32[]{:S(2)}, u32[]{:S(2)}) collective-permute-start(bf16[128,1664]{1,0:T(8,128)(2,1)} %get-tuple-element.320), channel_id=1, source_target_pairs={{0,4},{1,5},{2,6},{3,7},{4,0},{5,1},{6,2},{7,3},{8,12},{9,13},{10,... | collective-permute-start | bytes 1277960 | tf_op jit(solution)/shard_map/ppermute | solution.py:591
  301.8 28.6 %collective-permute-start.16 = (bf16[128,1664]{1,0:T(8,128)(2,1)}, bf16[128,1664]{1,0:T(8,128)(2,1)}, u32[]{:S(2)}, u32[]{:S(2)}) collective-permute-start(bf16[128,1664]{1,0:T(8,128)(2,1)} %get-tuple-element.318), channel_id=1, source_target_pairs={{0,2},{1,3},{2,0},{3,1},{4,6},{5,7},{6,4},{7,5},{8,10},{9,11},{10,... | collective-permute-start | bytes 1277960 | tf_op jit(solution)/shard_map/ppermute | solution.py:591
  334.7 5.9 %collective-permute-start.19 = (f32[64,128]{1,0:T(8,128)S(1)}, f32[64,128]{1,0:T(8,128)S(1)}, u32[]{:S(2)}, u32[]{:S(2)}) collective-permute-start(f32[64,128]{1,0:T(8,128)S(1)} %pad_bitcast_fusion.1), channel_id=1, source_target_pairs={{0,1},{1,0},{2,3},{3,2},{4,5},{5,4},{6,7},{7,6},{8,9},{9,8},{10,11... | collective-permute-start | bytes 98312 | tf_op jit(solution)/shard_map/ppermute | solution.py:591
  336.2 10.0 %collective-permute-start.26 = (bf16[128,256]{1,0:T(8,128)(2,1)S(1)}, bf16[128,256]{1,0:T(8,128)(2,1)S(1)}, u32[]{:S(2)}, u32[]{:S(2)}) collective-permute-start(bf16[128,256]{1,0:T(8,128)(2,1)S(1)} %get-tuple-element.341), channel_id=1, source_target_pairs={{0,24},{8,16},{16,8},{24,0},{1,25},{9,17},{17,9},{25,1},{2,26},{10... | collective-permute-start | bytes 196616 | tf_op jit(solution)/shard_map/ppermute | solution.py:591
  339.7 7.5 %collective-permute-start.25 = (bf16[128,256]{1,0:T(8,128)(2,1)S(1)}, bf16[128,256]{1,0:T(8,128)(2,1)S(1)}, u32[]{:S(2)}, u32[]{:S(2)}) collective-permute-start(bf16[128,256]{1,0:T(8,128)(2,1)S(1)} %get-tuple-element.342), channel_id=1, source_target_pairs={{0,16},{8,24},{16,0},{24,8},{1,17},{9,25},{17,1},{25,9},{2,18},{10... | collective-permute-start | bytes 196616 | tf_op jit(solution)/shard_map/ppermute | solution.py:591
  339.7 7.5 %collective-permute-start.24 = (bf16[128,256]{1,0:T(8,128)(2,1)S(1)}, bf16[128,256]{1,0:T(8,128)(2,1)S(1)}, u32[]{:S(2)}, u32[]{:S(2)}) collective-permute-start(bf16[128,256]{1,0:T(8,128)(2,1)S(1)} %get-tuple-element.340), channel_id=1, source_target_pairs={{0,8},{8,0},{16,24},{24,16},{1,9},{9,1},{17,25},{25,17},{2,10},{10... | collective-permute-start | bytes 196616 | tf_op jit(solution)/shard_map/ppermute | solution.py:591
  355.8 7.2 %collective-permute-start.23 = (f32[184,128]{1,0:T(8,128)S(1)}, f32[184,128]{1,0:T(8,128)S(1)}, u32[]{:S(2)}, u32[]{:S(2)}) collective-permute-start(f32[184,128]{1,0:T(8,128)S(1)} %add.244), channel_id=1, source_target_pairs={{0,16},{8,24},{16,0},{24,8},{1,17},{9,25},{17,1},{25,9},{2,18},{10... | collective-permute-start | bytes 282632 | tf_op jit(solution)/shard_map/ppermute | solution.py:591
  (75 other events, 737.7 us)
Sparse Core Ops, SparseCore 0:
  11.3 36.1 all-gather.4
  49.4 39.7 all-gather.6
  91.6 28.1 all-gather.8
  121.6 39.7 all-gather.10
  193.7 53.1 reduce-scatter.2
  250.6 81.0 reduce-scatter.4

commit v2 on v1

--- a/solution.py
+++ b/solution.py
@@ -512,8 +512,7 @@
         aliases = {19: 0}
     read = lambda i: (last - i, 0)
     read_cube = lambda i: (last - i, 0, 0)
-    tiles = lambda i: (steps - 1 - i, 0)
-    cubes = lambda i: (steps - 1 - i, 0, 0)
+    tiles, cubes = read, read_cube
     unit_spec = pl.BlockSpec((units, ROWS, width), cubes)
     out = pl.pallas_call(
         partial(bwd_kernel, heads, per_step),
@@ -729,15 +728,8 @@
 
     gain = out_gain[None]
     consts = (raw, aux, segrow, taps, bias, gain)
-    carry, mixed_parts, saved = None, [], []
-    for part in range(SPANS):
-        if part == SPANS - 1:
-            carry, shards = lax.optimization_barrier((carry, shards))
-        mixed_part, kept, carry = mixer_forward(*consts, carry, local_heads, FWD_CHUNKS, part, SPANS)
-        mixed_parts.append(mixed_part)
-        saved.append(kept)
-    mixed_parts, pair_grad = lax.optimization_barrier((mixed_parts, pair_grad))
-    mixed_low = jnp.concatenate(mixed_parts, axis=0)
+    mixed_low, saved, _ = mixer_forward(*consts, None, local_heads, FWD_CHUNKS, 0, 1)
+    mixed_low, pair_grad, shards = lax.optimization_barrier((mixed_low, pair_grad, shards))
     ff_sets += [lax.all_gather(shard, "batch", axis=0, tiled=True) for shard in shards[1:]]
 
     mixed_all = jnp.concatenate(
@@ -819,7 +811,7 @@
                 for rest in ff_last
             ]
         carry = mixer_backward(
-            mixed_grad, raw, aux, segrow, saved[part], taps, bias, gain, carry,
+            mixed_grad, raw, aux, segrow, saved, taps, bias, gain, carry,
             local_heads, BWD_CHUNKS, part, SPANS,
         )
     _, _, taps_grad, bias_grad, gain_grad, raw_low = carry

time: 377 us -> 368 us (0.976)
  matrix products: 85.3 us -> 72.6 us
  local copies, waits for them, and re-layouts: 26.2 us -> 30.4 us
    dot_general x27, matrix products: 85.3 us -> 72.6 us  [dot(): lax.dot_general(left, right, (dims, ((), ())), preferred_element_type=jnp...]
    pallas_call x2 -> x1, Pallas kernels: 33.4 us -> 29.9 us  [mixer_forward(): pl.pallas_call(partial(fwd_kernel, heads, per_step), grid=(steps,), in_sp...]
    unnamed x165 -> x162, local copies, waits for them, and re-layouts: 8.67 us -> 11.6 us
  transfers between devices with their start and end apart: 35 -> 35, of which waited for: 17 -> 19; matrix products, arithmetic and copies ran while one was open for 32% -> 31% of each run, Pallas kernels for 19% -> 18%
where the time goes in v2:
time: 368 us; the launch traced here: 364 us
  waiting for transfers between devices  104 us (28%)
  matrix products  72.6 us (20%)
  Pallas kernels  67.2 us (18%)
  starting transfers between devices  47.5 us (13%)
  local copies, waits for them, and re-layouts  30.4 us (8%)
  other arithmetic  26.5 us (7%)
  between operations  15.6 us (4%)
    dot_general x27, matrix products, dot(): lax.dot_general(left, right, (dims, ((), ())), preferred_element_type=jnp...  72.6 us
    ppermute x27, waiting for transfers between devices, swap(): return lax.ppermute(x, axis, [(i, i ^ bit) for i in range(size)])  53.3 us
    all_to_all x2, waiting for transfers between devices, exchange(): return lax.all_to_all(blocks, axis, split_axis=0, concat_axis=0, tiled=True)  46.3 us
    pallas_call x2, Pallas kernels, mixer_backward(): pl.pallas_call(partial(bwd_kernel, heads, per_step), grid=(steps,), in_sp...  37.3 us
    ppermute x27, starting transfers between devices, swap(): return lax.ppermute(x, axis, [(i, i ^ bit) for i in range(size)])  35.5 us
    pallas_call x1, Pallas kernels, mixer_forward(): pl.pallas_call(partial(fwd_kernel, heads, per_step), grid=(steps,), in_sp...  29.9 us
    unnamed x162, local copies, waits for them, and re-layouts  11.6 us
    all_to_all x2, starting transfers between devices, exchange(): return lax.all_to_all(blocks, axis, split_axis=0, concat_axis=0, tiled=True)  11.2 us
  transfers between devices with their start and end apart: 35, of which 19 were waited for; matrix products, arithmetic and copies ran while one was open for 31% of the time, Pallas kernels for 18%

profile of v2, /device:TPU:0, one launch (start us, length us, event | category | flops | bytes accessed | tf_op | source)
XLA Modules:
  0.0 364.1 jit_solution(16154338945341218250)
XLA Ops:
  8.3 2.7 broadcast_in_dim.17
  12.9 6.5 %all-to-all-start = ((bf16[4,256,1024]{2,1,0:T(8,128)(2,1)}), bf16[4,256,1024]{2,1,0:T(8,128)(2,1)S(1)}, u32[]{:S(2)}, u32[]{:S(2)}) async-start(bf16[4,256,1024]{2,1,0:T(8,128)(2,1)} %broadcast_in_dim.17), calls=%async_computation | async-start | bytes 4194304 | tf_op jit(solution)/shard_map/all_to_all | solution.py:594
  21.6 46.3 %all-to-all-done = bf16[4,256,1024]{2,1,0:T(8,128)(2,1)S(1)} async-done(((bf16[4,256,1024]{2,1,0:T(8,128)(2,1)}), bf16[4,256,1024]{2,1,0:T(8,128)(2,1)S(1)}, u32[]{:S(2)}, u32[]{:S(2)}) %all-to-all-start) | async-done | bytes 2097184 | tf_op jit(solution)/shard_map/all_to_all | solution.py:594
  69.0 3.3 collective-permute-start
  79.0 9.3 %fusion.125.raw_ref = f32[1024,1664]{1,0:T(8,128)} fusion(bf16[1024,1024]{1,0:T(8,128)(2,1)} %fusion.3, bf16[1024,1664]{1,0:T(8,128)(2,1)} %all-gather.5.cloned.1.call-done), kind=kOutput, calls=%fused_computation.229 | convolution fusion | flops 3489660928 | bytes 12320768 | tf_op jit(solution)/shard_map/dot_general | solution.py:585
  89.9 29.9 %mixer_forward.1 = (bf16[1024,256]{1,0:T(8,128)(2,1)S(1)}, f32[1024,1280]{1,0:T(8,128)}, f32[1024,256]{1,0:T(8,128)}, f32[32,128,128]{2,1,0:T(8,128)}, f32[32,12...) custom-call(f32[1024,1664]{1,0:T(8,128)} %fusion.125.raw_ref, ...), custom_call_target="tpu_custom_call" | custom-call | tf_op jit(solution)/shard_map/mixer_forward/pallas_call | solution.py:447
  121.1 3.3 collective-permute-start.7
  129.6 6.8 %collective-permute-done.6 = bf16[256,256]{1,0:T(8,128)(2,1)} collective-permute-done((bf16[256,256]{1,0:T(8,128)(2,1)}, bf16[256,256]{1,0:T(8,128)(2,1)}, u32[]{:S(2)}, u32[]{:S(2)}) %collective-permute-start.6) | collective-permute-done | bytes 131104 | tf_op jit(solution)/shard_map/ppermute | solution.py:590
  136.5 2.8 multiply_reduce_fusion.3
  141.5 2.7 multiply_convert_fusion.12
  147.1 6.7 %collective-permute-done.8 = bf16[256,1024]{1,0:T(8,128)(2,1)S(1)} collective-permute-done((bf16[256,1024]{1,0:T(8,128)(2,1)S(1)}, bf16[256,1024]{1,0:T(8,128)(2,1)S(1)}, u32[]{:S(2)}, u32[]{:S(2)}) %collective-permute-start.8) | collective-permute-done | bytes 524320 | tf_op jit(solution)/shard_map/ppermute | solution.py:590
  154.8 2.7 multiply_convert_fusion.9
  162.1 3.0 fusion.10
  187.3 2.5 fusion.115
  190.7 2.5 collective-permute-start.11
  195.3 4.4 %collective-permute-done.10 = bf16[256,256]{1,0:T(8,128)(2,1)S(1)} collective-permute-done((bf16[256,256]{1,0:T(8,128)(2,1)S(1)}, bf16[256,256]{1,0:T(8,128)(2,1)S(1)}, u32[]{:S(2)}, u32[]{:S(2)}) %collective-permute-start.10) | collective-permute-done | bytes 131104 | tf_op jit(solution)/shard_map/ppermute | solution.py:590
  199.8 3.4 collective-permute-done.11
  205.3 3.2 fusion.37
  208.5 18.3 %mixer_backward.2 = (bf16[1024,1664]{1,0:T(8,128)(2,1)}, f32[4,1280]{1,0:T(4,128)S(1)}, f32[1,128]{1,0:T(1,128)S(1)}, f32[1,128]{1,0:T(1,128)S(1)}, f32[2,128,128]{2,1,0:T(8,128)S(1)}, /*index=5*/f32[8,1280]{1,0:T(8,128)S(1)}) custom-call(bf16[1024,256]{1,0:T(8,128)(2,1)S(1)} %constant_dynamic-update-slice_fusion.9.grad_ref, f32[1024,1664]{1,0:T(8,128)} %fusion.125.raw_ref, ...), custom_call_target="tpu_custom_call" | custom-call | tf_op jit(solution)/shard_map/mixer_backward/pallas_call | solution.py:517
  226.8 2.4 convolution_convert_fusion.5
  233.0 3.2 pad_maximum_fusion
  237.5 2.4 collective-permute-start.14
  243.2 19.0 %mixer_backward.3 = (bf16[1024,1664]{1,0:T(8,128)(2,1)}, f32[4,1280]{1,0:T(4,128)S(1)}, f32[1,128]{1,0:T(1,128)S(1)}, f32[1,128]{1,0:T(1,128)S(1)}, f32[2,128,128]{2,1,0:T(8,128)}, /*index=5*/f32[8,1280]{1,0:T(8,128)}) custom-call(bf16[1024,256]{1,0:T(8,128)(2,1)S(1)} %constant_dynamic-update-slice_fusion.9.grad_ref, ...), custom_call_target="tpu_custom_call", output_to_operand_aliasing={{0}: (19, {})} | custom-call | tf_op jit(solution)/shard_map/mixer_backward/pallas_call | solution.py:517
  266.5 7.5 %convolution_convert_fusion.3 = bf16[1024,1024]{1,0:T(8,128)(2,1)} fusion(bf16[1024,1664]{1,0:T(8,128)(2,1)} %get-tuple-element.195, bf16[1024,1664]{1,0:T(8,128)(2,1)S(1)} %copy-done.65), kind=kOutput, calls=%fused_computation.30 | convolution fusion | flops 3490709504 | bytes 8912896 | tf_op jit(solution)/shard_map/dot_general | solution.py:585
  274.1 3.4 convolution_convert_fusion.2
  279.6 4.8 %all-to-all-start.1 = ((bf16[4,256,1024]{2,1,0:T(8,128)(2,1)}), bf16[4,256,1024]{2,1,0:T(8,128)(2,1)}, u32[]{:S(2)}, u32[]{:S(2)}) async-start(bf16[4,256,1024]{2,1,0:T(8,128)(2,1)} %bitcast.104), calls=%async_computation.3 | async-start | bytes 4194304 | tf_op jit(solution)/shard_map/all_to_all | solution.py:594
  285.1 4.9 %add_convert_fusion = bf16[512,1664]{1,0:T(8,128)(2,1)S(1)} fusion(bf16[512,1664]{1,0:T(8,128)(2,1)} %collective-permute-done.15, bf16[1024,1664]{1,0:T(8,128)(2,1)} %get-tuple-element.195, pred[]{:T(512)S(6)} %eq.61, bf16[1024,128]{1,0:T(8,128)(2,1)S(1)} %copy-done.37, bf16[1024,128]{1,0:T(8,128)(2,1)S(1)} %copy-done.39, ...), kind=kOutput, calls=%fused_computation.12 | convolution fusion | flops 1756299264 | bytes 8912897 | tf_op jit(solution)/shard_map/dot_general | solution.py:585
  299.1 3.0 add_convert_fusion.1
  302.1 11.1 %collective-permute-done.16 = bf16[128,1664]{1,0:T(8,128)(2,1)} collective-permute-done((bf16[128,1664]{1,0:T(8,128)(2,1)}, bf16[128,1664]{1,0:T(8,128)(2,1)}, u32[]{:S(2)}, u32[]{:S(2)}) %collective-permute-start.16) | collective-permute-done | bytes 426016 | tf_op jit(solution)/shard_map/ppermute | solution.py:590
  313.2 9.6 %collective-permute-done.18 = bf16[128,1664]{1,0:T(8,128)(2,1)} collective-permute-done((bf16[128,1664]{1,0:T(8,128)(2,1)}, bf16[128,1664]{1,0:T(8,128)(2,1)}, u32[]{:S(2)}, u32[]{:S(2)}) %collective-permute-start.18) | collective-permute-done | bytes 426016 | tf_op jit(solution)/shard_map/ppermute | solution.py:590
  333.8 2.9 collective-permute-done.20
  345.7 3.0 collective-permute-start.23
  (342 shorter events, 110.8 us)
Async XLA Ops:
  7.3 71.7 %all-gather.5.cloned.1.call-start = ((), (), s32[]{:S(2)}) async-start(), calls=%async_computation.4 | async-start | bytes 3833856 | tf_op jit(solution)/shard_map/all_gather | solution.py:687
  11.9 78.0 %all-gather.7.cloned.1.call-start = ((), (), s32[]{:S(2)}) async-start(), calls=%async_computation.5 | async-start | bytes 5308416 | tf_op jit(solution)/shard_map/all_gather | solution.py:693
  12.9 55.0 %all-to-all-start = ((bf16[4,256,1024]{2,1,0:T(8,128)(2,1)}), bf16[4,256,1024]{2,1,0:T(8,128)(2,1)S(1)}, u32[]{:S(2)}, u32[]{:S(2)}) async-start(bf16[4,256,1024]{2,1,0:T(8,128)(2,1)} %broadcast_in_dim.17), calls=%async_computation | async-start | bytes 4194304 | tf_op jit(solution)/shard_map/all_to_all | solution.py:594
  19.4 109.9 %all-gather.9.cloned.1.call-start = ((), (), s32[]{:S(2)}) async-start(), calls=%async_computation.6 | async-start | bytes 2359296 | tf_op jit(solution)/shard_map/all_gather | solution.py:724
  67.9 7.3 %collective-permute-start.2 = (bf16[128,256]{0,1:T(8,128)(2,1)S(1)}, bf16[128,256]{0,1:T(8,128)(2,1)S(1)}, u32[]{:S(2)}, u32[]{:S(2)}) collective-permute-start(bf16[128,256]{0,1:T(8,128)(2,1)S(1)} %bitcast.117), channel_id=1, source_target_pairs={{0,24},{8,16},{16,8},{24,0},{1,25},{9,17},{17,9},{25,1},{2,26},{10... | collective-permute-start | bytes 196616 | tf_op jit(solution)/shard_map/ppermute | solution.py:590
  69.0 6.4 %collective-permute-start.1 = (bf16[128,256]{0,1:T(8,128)(2,1)S(1)}, bf16[128,256]{0,1:T(8,128)(2,1)S(1)}, u32[]{:S(2)}, u32[]{:S(2)}) collective-permute-start(bf16[128,256]{0,1:T(8,128)(2,1)S(1)} %bitcast.118), channel_id=1, source_target_pairs={{0,16},{8,24},{16,0},{24,8},{1,17},{9,25},{17,1},{25,9},{2,18},{10... | collective-permute-start | bytes 196616 | tf_op jit(solution)/shard_map/ppermute | solution.py:590
  69.0 6.4 %collective-permute-start = (bf16[128,256]{0,1:T(8,128)(2,1)S(1)}, bf16[128,256]{0,1:T(8,128)(2,1)S(1)}, u32[]{:S(2)}, u32[]{:S(2)}) collective-permute-start(bf16[128,256]{0,1:T(8,128)(2,1)S(1)} %bitcast.119), channel_id=1, source_target_pairs={{0,8},{8,0},{16,24},{24,16},{1,9},{9,1},{17,25},{25,17},{2,10},{10... | collective-permute-start | bytes 196616 | tf_op jit(solution)/shard_map/ppermute | solution.py:590
  76.1 85.9 %all-gather.11.cloned.1.call-start = ((), (), s32[]{:S(2)}) async-start(), calls=%async_computation.7 | async-start | bytes 5308416 | tf_op jit(solution)/shard_map/all_gather | solution.py:733
  76.6 43.2 %collective-permute-start.3 = (bf16[256,1024]{1,0:T(8,128)(2,1)}, bf16[256,1024]{1,0:T(8,128)(2,1)}, u32[]{:S(2)}, u32[]{:S(2)}) collective-permute-start(bf16[256,1024]{1,0:T(8,128)(2,1)} %param.20), channel_id=1, source_target_pairs={{0,8},{8,0},{16,24},{24,16},{1,9},{9,1},{17,25},{25,17},{2,10},{10... | collective-permute-start | bytes 1572872 | tf_op jit(solution)/shard_map/ppermute | solution.py:590
  77.8 42.0 %collective-permute-start.4 = (bf16[128,2304]{0,1:T(8,128)(2,1)}, bf16[128,2304]{0,1:T(8,128)(2,1)}, u32[]{:S(2)}, u32[]{:S(2)}) collective-permute-start(bf16[128,2304]{0,1:T(8,128)(2,1)} %fusion.90), channel_id=1, source_target_pairs={{0,16},{8,24},{16,0},{24,8},{1,17},{9,25},{17,1},{25,9},{2,18},{10... | collective-permute-start | bytes 1769480 | tf_op jit(solution)/shard_map/ppermute | solution.py:590
  119.8 117.7 %reduce-scatter.3.cloned.1.call-start = ((), (), s32[]{:S(2)}) async-start(), calls=%async_computation.8 | async-start | bytes 5308416 | tf_op jit(solution)/shard_map/reduce_scatter | solution.py:791
  121.1 8.5 %collective-permute-start.7 = (bf16[256,256]{1,0:T(8,128)(2,1)}, bf16[256,256]{1,0:T(8,128)(2,1)}, u32[]{:S(2)}, u32[]{:S(2)}) collective-permute-start(bf16[256,256]{1,0:T(8,128)(2,1)} %get-tuple-element.311), channel_id=1, source_target_pairs={{0,24},{8,16},{16,8},{24,0},{1,25},{9,17},{17,9},{25,1},{2,26},{10... | collective-permute-start | bytes 393224 | tf_op jit(solution)/shard_map/ppermute | solution.py:590
  124.4 12.0 %collective-permute-start.6 = (bf16[256,256]{1,0:T(8,128)(2,1)}, bf16[256,256]{1,0:T(8,128)(2,1)}, u32[]{:S(2)}, u32[]{:S(2)}) collective-permute-start(bf16[256,256]{1,0:T(8,128)(2,1)} %get-tuple-element.312), channel_id=1, source_target_pairs={{0,16},{8,24},{16,0},{24,8},{1,17},{9,25},{17,1},{25,9},{2,18},{10... | collective-permute-start | bytes 393224 | tf_op jit(solution)/shard_map/ppermute | solution.py:590
  124.4 12.0 %collective-permute-start.5 = (bf16[256,256]{1,0:T(8,128)(2,1)}, bf16[256,256]{1,0:T(8,128)(2,1)}, u32[]{:S(2)}, u32[]{:S(2)}) collective-permute-start(bf16[256,256]{1,0:T(8,128)(2,1)} %get-tuple-element.313), channel_id=1, source_target_pairs={{0,8},{8,0},{16,24},{24,16},{1,9},{9,1},{17,25},{25,17},{2,10},{10... | collective-permute-start | bytes 393224 | tf_op jit(solution)/shard_map/ppermute | solution.py:590
  140.4 13.4 %collective-permute-start.8 = (bf16[256,1024]{1,0:T(8,128)(2,1)S(1)}, bf16[256,1024]{1,0:T(8,128)(2,1)S(1)}, u32[]{:S(2)}, u32[]{:S(2)}) collective-permute-start(bf16[256,1024]{1,0:T(8,128)(2,1)S(1)} %multiply_convert_fusion), channel_id=1, source_target_pairs={{0,8},{8,0},{16,24},{24,16},{1,9},{9,1},{17,25},{25,17},{2,10},{10... | collective-permute-start | bytes 1572872 | tf_op jit(solution)/shard_map/ppermute | solution.py:590
  169.2 14.3 %collective-permute-start.9 = (bf16[256,1024]{1,0:T(8,128)(2,1)}, bf16[256,1024]{1,0:T(8,128)(2,1)S(1)}, u32[]{:S(2)}, u32[]{:S(2)}) collective-permute-start(bf16[256,1024]{1,0:T(8,128)(2,1)} %fusion.38), channel_id=1, source_target_pairs={{0,8},{8,0},{16,24},{24,16},{1,9},{9,1},{17,25},{25,17},{2,10},{10... | collective-permute-start | bytes 1572872 | tf_op jit(solution)/shard_map/ppermute | solution.py:590
  183.5 142.6 %reduce-scatter.5.cloned.1.call-start = ((), (), s32[]{:S(2)}) async-start(), calls=%async_computation.9 | async-start | bytes 7667712 | tf_op jit(solution)/shard_map/reduce_scatter | solution.py:810
  190.7 12.5 %collective-permute-start.11 = (bf16[256,256]{1,0:T(8,128)(2,1)S(1)}, bf16[256,256]{1,0:T(8,128)(2,1)S(1)}, u32[]{:S(2)}, u32[]{:S(2)}) collective-permute-start(bf16[256,256]{1,0:T(8,128)(2,1)S(1)} %get-tuple-element.307), channel_id=1, source_target_pairs={{0,16},{8,24},{16,0},{24,8},{1,17},{9,25},{17,1},{25,9},{2,18},{10... | collective-permute-start | bytes 393224 | tf_op jit(solution)/shard_map/ppermute | solution.py:590
  193.2 6.6 %collective-permute-start.10 = (bf16[256,256]{1,0:T(8,128)(2,1)S(1)}, bf16[256,256]{1,0:T(8,128)(2,1)S(1)}, u32[]{:S(2)}, u32[]{:S(2)}) collective-permute-start(bf16[256,256]{1,0:T(8,128)(2,1)S(1)} %get-tuple-element.309), channel_id=1, source_target_pairs={{0,8},{8,0},{16,24},{24,16},{1,9},{9,1},{17,25},{25,17},{2,10},{10... | collective-permute-start | bytes 393224 | tf_op jit(solution)/shard_map/ppermute | solution.py:590
  194.7 8.5 %collective-permute-start.12 = (bf16[256,256]{1,0:T(8,128)(2,1)S(1)}, bf16[256,256]{1,0:T(8,128)(2,1)S(1)}, u32[]{:S(2)}, u32[]{:S(2)}) collective-permute-start(bf16[256,256]{1,0:T(8,128)(2,1)S(1)} %get-tuple-element.306), channel_id=1, source_target_pairs={{0,24},{8,16},{16,8},{24,0},{1,25},{9,17},{17,9},{25,1},{2,26},{10... | collective-permute-start | bytes 393224 | tf_op jit(solution)/shard_map/ppermute | solution.py:590
  237.5 28.9 %collective-permute-start.14 = (bf16[128,2304]{1,0:T(8,128)(2,1)}, bf16[128,2304]{1,0:T(8,128)(2,1)}, u32[]{:S(2)}, u32[]{:S(2)}) collective-permute-start(bf16[128,2304]{1,0:T(8,128)(2,1)} %reduce-scatter.3.cloned.1.call-done), channel_id=1, source_target_pairs={{0,16},{8,24},{16,0},{24,8},{1,17},{9,25},{17,1},{25,9},{2,18},{10... | collective-permute-start | bytes 1769480 | tf_op jit(solution)/shard_map/ppermute | solution.py:590
  240.0 24.4 %collective-permute-start.13 = (bf16[256,1024]{1,0:T(8,128)(2,1)}, bf16[256,1024]{1,0:T(8,128)(2,1)}, u32[]{:S(2)}, u32[]{:S(2)}) collective-permute-start(bf16[256,1024]{1,0:T(8,128)(2,1)} %fusion.37), channel_id=1, source_target_pairs={{0,8},{8,0},{16,24},{24,16},{1,9},{9,1},{17,25},{25,17},{2,10},{10... | collective-permute-start | bytes 1572872 | tf_op jit(solution)/shard_map/ppermute | solution.py:590
  277.5 7.6 %collective-permute-start.15 = (bf16[512,1664]{1,0:T(8,128)(2,1)}, bf16[512,1664]{1,0:T(8,128)(2,1)}, u32[]{:S(2)}, u32[]{:S(2)}) collective-permute-start(bf16[512,1664]{1,0:T(8,128)(2,1)} %convolution_convert_fusion.2), channel_id=1, source_target_pairs={{0,1},{1,0},{2,3},{3,2},{4,5},{5,4},{6,7},{7,6},{8,9},{9,8},{10,11... | collective-permute-start | bytes 5111816 | tf_op jit(solution)/shard_map/ppermute | solution.py:590
  279.6 61.4 %all-to-all-start.1 = ((bf16[4,256,1024]{2,1,0:T(8,128)(2,1)}), bf16[4,256,1024]{2,1,0:T(8,128)(2,1)}, u32[]{:S(2)}, u32[]{:S(2)}) async-start(bf16[4,256,1024]{2,1,0:T(8,128)(2,1)} %bitcast.104), calls=%async_computation.3 | async-start | bytes 4194304 | tf_op jit(solution)/shard_map/all_to_all | solution.py:594
  291.2 22.0 %collective-permute-start.16 = (bf16[128,1664]{1,0:T(8,128)(2,1)}, bf16[128,1664]{1,0:T(8,128)(2,1)}, u32[]{:S(2)}, u32[]{:S(2)}) collective-permute-start(bf16[128,1664]{1,0:T(8,128)(2,1)} %get-tuple-element.292), channel_id=1, source_target_pairs={{0,2},{1,3},{2,0},{3,1},{4,6},{5,7},{6,4},{7,5},{8,10},{9,11},{10,... | collective-permute-start | bytes 1277960 | tf_op jit(solution)/shard_map/ppermute | solution.py:590
  292.6 30.2 %collective-permute-start.18 = (bf16[128,1664]{1,0:T(8,128)(2,1)}, bf16[128,1664]{1,0:T(8,128)(2,1)}, u32[]{:S(2)}, u32[]{:S(2)}) collective-permute-start(bf16[128,1664]{1,0:T(8,128)(2,1)} %get-tuple-element.293), channel_id=1, source_target_pairs={{0,6},{1,7},{2,4},{3,5},{4,2},{5,3},{6,0},{7,1},{8,14},{9,15},{10,... | collective-permute-start | bytes 1277960 | tf_op jit(solution)/shard_map/ppermute | solution.py:590
  294.1 28.7 %collective-permute-start.17 = (bf16[128,1664]{1,0:T(8,128)(2,1)}, bf16[128,1664]{1,0:T(8,128)(2,1)}, u32[]{:S(2)}, u32[]{:S(2)}) collective-permute-start(bf16[128,1664]{1,0:T(8,128)(2,1)} %get-tuple-element.294), channel_id=1, source_target_pairs={{0,4},{1,5},{2,6},{3,7},{4,0},{5,1},{6,2},{7,3},{8,12},{9,13},{10,... | collective-permute-start | bytes 1277960 | tf_op jit(solution)/shard_map/ppermute | solution.py:590
  327.1 5.6 %collective-permute-start.19 = (f32[64,128]{1,0:T(8,128)S(1)}, f32[64,128]{1,0:T(8,128)S(1)}, u32[]{:S(2)}, u32[]{:S(2)}) collective-permute-start(f32[64,128]{1,0:T(8,128)S(1)} %pad_bitcast_fusion.1), channel_id=1, source_target_pairs={{0,1},{1,0},{2,3},{3,2},{4,5},{5,4},{6,7},{7,6},{8,9},{9,8},{10,11... | collective-permute-start | bytes 98312 | tf_op jit(solution)/shard_map/ppermute | solution.py:590
  328.5 8.7 %collective-permute-start.24 = (bf16[128,256]{1,0:T(8,128)(2,1)S(1)}, bf16[128,256]{1,0:T(8,128)(2,1)S(1)}, u32[]{:S(2)}, u32[]{:S(2)}) collective-permute-start(bf16[128,256]{1,0:T(8,128)(2,1)S(1)} %get-tuple-element.314), channel_id=1, source_target_pairs={{0,8},{8,0},{16,24},{24,16},{1,9},{9,1},{17,25},{25,17},{2,10},{10... | collective-permute-start | bytes 196616 | tf_op jit(solution)/shard_map/ppermute | solution.py:590
  330.3 7.0 %collective-permute-start.26 = (bf16[128,256]{1,0:T(8,128)(2,1)S(1)}, bf16[128,256]{1,0:T(8,128)(2,1)S(1)}, u32[]{:S(2)}, u32[]{:S(2)}) collective-permute-start(bf16[128,256]{1,0:T(8,128)(2,1)S(1)} %get-tuple-element.315), channel_id=1, source_target_pairs={{0,24},{8,16},{16,8},{24,0},{1,25},{9,17},{17,9},{25,1},{2,26},{10... | collective-permute-start | bytes 196616 | tf_op jit(solution)/shard_map/ppermute | solution.py:590
  332.6 6.7 %collective-permute-start.25 = (bf16[128,256]{1,0:T(8,128)(2,1)S(1)}, bf16[128,256]{1,0:T(8,128)(2,1)S(1)}, u32[]{:S(2)}, u32[]{:S(2)}) collective-permute-start(bf16[128,256]{1,0:T(8,128)(2,1)S(1)} %get-tuple-element.316), channel_id=1, source_target_pairs={{0,16},{8,24},{16,0},{24,8},{1,17},{9,25},{17,1},{25,9},{2,18},{10... | collective-permute-start | bytes 196616 | tf_op jit(solution)/shard_map/ppermute | solution.py:590
  345.7 7.7 %collective-permute-start.23 = (f32[184,128]{1,0:T(8,128)S(1)}, f32[184,128]{1,0:T(8,128)S(1)}, u32[]{:S(2)}, u32[]{:S(2)}) collective-permute-start(f32[184,128]{1,0:T(8,128)S(1)} %add.244), channel_id=1, source_target_pairs={{0,16},{8,24},{16,0},{24,8},{1,17},{9,25},{17,1},{25,9},{2,18},{10... | collective-permute-start | bytes 282632 | tf_op jit(solution)/shard_map/ppermute | solution.py:590
  (74 other events, 705.5 us)
Sparse Core Ops, SparseCore 0:
  12.0 36.1 all-gather.4
  50.1 39.7 all-gather.6
  92.3 28.1 all-gather.8
  122.3 39.7 all-gather.10
  183.6 53.8 reduce-scatter.2
  241.2 73.2 reduce-scatter.4

commit v3 on v2

--- a/solution.py
+++ b/solution.py
@@ -724,12 +724,14 @@
     out_all = lax.all_gather(
         jnp.concatenate(out_shards, axis=1), "batch", axis=0, tiled=True
     )
-    raw, ff_sets[0] = lax.optimization_barrier((dot(rows_in, proj_w), ff_sets[0]))
+    raw = dot(rows_in, proj_w)
 
     gain = out_gain[None]
     consts = (raw, aux, segrow, taps, bias, gain)
     mixed_low, saved, _ = mixer_forward(*consts, None, local_heads, FWD_CHUNKS, 0, 1)
-    mixed_low, pair_grad, shards = lax.optimization_barrier((mixed_low, pair_grad, shards))
+    mixed_low, pair_grad, shards, ff_sets[0] = lax.optimization_barrier(
+        (mixed_low, pair_grad, shards, ff_sets[0])
+    )
     ff_sets += [lax.all_gather(shard, "batch", axis=0, tiled=True) for shard in shards[1:]]
 
     mixed_all = jnp.concatenate(

time: 368 us -> 378 us (1.027)
  waiting for transfers between devices: 104 us -> 116 us
    all_gather x1, waiting for transfers between devices: 1.65 us -> 9.9 us  [body(): lax.all_gather(shard, 'batch', axis=0, tiled=True)]
    ppermute x27, waiting for transfers between devices: 53.3 us -> 58.1 us  [swap(): return lax.ppermute(x, axis, [(i, i ^ bit) for i in range(size)])]
    unnamed x162 -> x168, local copies, waits for them, and re-layouts: 11.6 us -> 10.8 us
  transfers between devices with their start and end apart: 35 -> 35, of which waited for: 19 -> 17; matrix products, arithmetic and copies ran while one was open for 31% -> 27% of each run, Pallas kernels for 18% -> 18%
where the time goes in v3:
time: 378 us; the launch traced here: 374 us
  waiting for transfers between devices  116 us (31%)
  matrix products  71.6 us (19%)
  Pallas kernels  67.2 us (18%)
  starting transfers between devices  47.6 us (13%)
  local copies, waits for them, and re-layouts  29.6 us (8%)
  other arithmetic  26.7 us (7%)
  between operations  15.7 us (4%)
    dot_general x27, matrix products, dot(): lax.dot_general(left, right, (dims, ((), ())), preferred_element_type=jnp...  71.6 us
    ppermute x27, waiting for transfers between devices, swap(): return lax.ppermute(x, axis, [(i, i ^ bit) for i in range(size)])  58.1 us
    all_to_all x2, waiting for transfers between devices, exchange(): return lax.all_to_all(blocks, axis, split_axis=0, concat_axis=0, tiled=True)  46.3 us
    pallas_call x2, Pallas kernels, mixer_backward(): pl.pallas_call(partial(bwd_kernel, heads, per_step), grid=(steps,), in_sp...  37.3 us
    ppermute x27, starting transfers between devices, swap(): return lax.ppermute(x, axis, [(i, i ^ bit) for i in range(size)])  35.6 us
    pallas_call x1, Pallas kernels, mixer_forward(): pl.pallas_call(partial(fwd_kernel, heads, per_step), grid=(steps,), in_sp...  29.9 us
    all_to_all x2, starting transfers between devices, exchange(): return lax.all_to_all(blocks, axis, split_axis=0, concat_axis=0, tiled=True)  11.2 us
    unnamed x168, local copies, waits for them, and re-layouts  10.8 us
  transfers between devices with their start and end apart: 35, of which 17 were waited for; matrix products, arithmetic and copies ran while one was open for 27% of the time, Pallas kernels for 18%

profile of v3, /device:TPU:0, one launch (start us, length us, event | category | flops | bytes accessed | tf_op | source)
XLA Modules:
  0.0 373.9 jit_solution(8346876861107641846)
XLA Ops:
  8.3 2.7 broadcast_in_dim.17
  12.9 6.5 %all-to-all-start = ((bf16[4,256,1024]{2,1,0:T(8,128)(2,1)}), bf16[4,256,1024]{2,1,0:T(8,128)(2,1)S(1)}, u32[]{:S(2)}, u32[]{:S(2)}) async-start(bf16[4,256,1024]{2,1,0:T(8,128)(2,1)} %broadcast_in_dim.17), calls=%async_computation | async-start | bytes 4194304 | tf_op jit(solution)/shard_map/all_to_all | solution.py:594
  21.6 46.3 %all-to-all-done = bf16[4,256,1024]{2,1,0:T(8,128)(2,1)S(1)} async-done(((bf16[4,256,1024]{2,1,0:T(8,128)(2,1)}), bf16[4,256,1024]{2,1,0:T(8,128)(2,1)S(1)}, u32[]{:S(2)}, u32[]{:S(2)}) %all-to-all-start) | async-done | bytes 2097184 | tf_op jit(solution)/shard_map/all_to_all | solution.py:594
  69.0 3.3 collective-permute-start
  79.0 9.3 %fusion.125.raw_ref = f32[1024,1664]{1,0:T(8,128)} fusion(bf16[1024,1024]{1,0:T(8,128)(2,1)} %fusion.3, bf16[1024,1664]{1,0:T(8,128)(2,1)} %all-gather.5.cloned.1.call-done), kind=kOutput, calls=%fused_computation.230 | convolution fusion | flops 3489660928 | bytes 12320768 | tf_op jit(solution)/shard_map/dot_general | solution.py:585
  88.3 29.9 %mixer_forward.1 = (bf16[1024,256]{1,0:T(8,128)(2,1)S(1)}, f32[1024,1280]{1,0:T(8,128)}, f32[1024,256]{1,0:T(8,128)}, f32[32,128,128]{2,1,0:T(8,128)}, f32[32,12...) custom-call(f32[1024,1664]{1,0:T(8,128)} %fusion.125.raw_ref, ...), custom_call_target="tpu_custom_call" | custom-call | tf_op jit(solution)/shard_map/mixer_forward/pallas_call | solution.py:447
  127.7 4.1 %collective-permute-done.6 = bf16[256,256]{1,0:T(8,128)(2,1)} collective-permute-done((bf16[256,256]{1,0:T(8,128)(2,1)}, bf16[256,256]{1,0:T(8,128)(2,1)}, u32[]{:S(2)}, u32[]{:S(2)}) %collective-permute-start.6) | collective-permute-done | bytes 131104 | tf_op jit(solution)/shard_map/ppermute | solution.py:590
  131.9 2.8 multiply_reduce_fusion.3
  136.9 2.7 multiply_convert_fusion.12
  140.6 7.5 %collective-permute-done.8 = bf16[256,1024]{1,0:T(8,128)(2,1)S(1)} collective-permute-done((bf16[256,1024]{1,0:T(8,128)(2,1)S(1)}, bf16[256,1024]{1,0:T(8,128)(2,1)S(1)}, u32[]{:S(2)}, u32[]{:S(2)}) %collective-permute-start.8) | collective-permute-done | bytes 524320 | tf_op jit(solution)/shard_map/ppermute | solution.py:590
  149.2 3.0 multiply_convert_fusion.9
  152.1 9.9 %all-gather.11.cloned.1.call-done = bf16[1024,2304]{0,1:T(8,128)(2,1)} async-done(((bf16[128,2304]{0,1:T(8,128)(2,1)}), bf16[1024,2304]{0,1:T(8,128)(2,1)}) %all-gather.11.cloned.1.call-update) | async-done | bytes 4718608 | tf_op jit(solution)/shard_map/all_gather | solution.py:735
  162.0 3.0 fusion.6
  165.1 2.7 multiply_convert_fusion.5
  185.2 8.1 %collective-permute-done.9 = bf16[256,1024]{1,0:T(8,128)(2,1)S(1)} collective-permute-done((bf16[256,1024]{1,0:T(8,128)(2,1)}, bf16[256,1024]{1,0:T(8,128)(2,1)S(1)}, u32[]{:S(2)}, u32[]{:S(2)}) %collective-permute-start.9) | collective-permute-done | bytes 524320 | tf_op jit(solution)/shard_map/ppermute | solution.py:590
  197.2 2.6 fusion.115
  205.2 4.4 %collective-permute-done.10 = bf16[256,256]{1,0:T(8,128)(2,1)S(1)} collective-permute-done((bf16[256,256]{1,0:T(8,128)(2,1)S(1)}, bf16[256,256]{1,0:T(8,128)(2,1)S(1)}, u32[]{:S(2)}, u32[]{:S(2)}) %collective-permute-start.10) | collective-permute-done | bytes 131104 | tf_op jit(solution)/shard_map/ppermute | solution.py:590
  209.7 3.5 collective-permute-done.11
  215.2 3.2 fusion.38
  218.4 18.4 %mixer_backward.2 = (bf16[1024,1664]{1,0:T(8,128)(2,1)}, f32[4,1280]{1,0:T(4,128)S(1)}, f32[1,128]{1,0:T(1,128)S(1)}, f32[1,128]{1,0:T(1,128)S(1)}, f32[2,128,128]{2,1,0:T(8,128)S(1)}, /*index=5*/f32[8,1280]{1,0:T(8,128)S(1)}) custom-call(bf16[1024,256]{1,0:T(8,128)(2,1)S(1)} %constant_dynamic-update-slice_fusion.9.grad_ref, f32[1024,1664]{1,0:T(8,128)} %fusion.125.raw_ref, ...), custom_call_target="tpu_custom_call" | custom-call | tf_op jit(solution)/shard_map/mixer_backward/pallas_call | solution.py:517
  236.8 2.5 convolution_convert_fusion.5
  243.0 3.2 pad_maximum_fusion
  253.1 19.0 %mixer_backward.3 = (bf16[1024,1664]{1,0:T(8,128)(2,1)}, f32[4,1280]{1,0:T(4,128)S(1)}, f32[1,128]{1,0:T(1,128)S(1)}, f32[1,128]{1,0:T(1,128)S(1)}, f32[2,128,128]{2,1,0:T(8,128)}, /*index=5*/f32[8,1280]{1,0:T(8,128)}) custom-call(bf16[1024,256]{1,0:T(8,128)(2,1)S(1)} %constant_dynamic-update-slice_fusion.9.grad_ref, ...), custom_call_target="tpu_custom_call", output_to_operand_aliasing={{0}: (19, {})} | custom-call | tf_op jit(solution)/shard_map/mixer_backward/pallas_call | solution.py:517
  276.3 7.5 %convolution_convert_fusion.3 = bf16[1024,1024]{1,0:T(8,128)(2,1)} fusion(bf16[1024,1664]{1,0:T(8,128)(2,1)} %get-tuple-element.193, bf16[1024,1664]{1,0:T(8,128)(2,1)S(1)} %copy-done.66), kind=kOutput, calls=%fused_computation.30 | convolution fusion | flops 3490709504 | bytes 8912896 | tf_op jit(solution)/shard_map/dot_general | solution.py:585
  284.0 3.4 convolution_convert_fusion.2
  289.5 4.8 %all-to-all-start.1 = ((bf16[4,256,1024]{2,1,0:T(8,128)(2,1)}), bf16[4,256,1024]{2,1,0:T(8,128)(2,1)}, u32[]{:S(2)}, u32[]{:S(2)}) async-start(bf16[4,256,1024]{2,1,0:T(8,128)(2,1)} %bitcast.104), calls=%async_computation.3 | async-start | bytes 4194304 | tf_op jit(solution)/shard_map/all_to_all | solution.py:594
  295.0 4.9 %add_convert_fusion = bf16[512,1664]{1,0:T(8,128)(2,1)S(1)} fusion(bf16[512,1664]{1,0:T(8,128)(2,1)} %collective-permute-done.15, bf16[1024,1664]{1,0:T(8,128)(2,1)} %get-tuple-element.193, pred[]{:T(512)S(6)} %eq.61, bf16[1024,128]{1,0:T(8,128)(2,1)S(1)} %copy-done.38, bf16[1024,128]{1,0:T(8,128)(2,1)S(1)} %copy-done.40, ...), kind=kOutput, calls=%fused_computation.12 | convolution fusion | flops 1756299264 | bytes 8912897 | tf_op jit(solution)/shard_map/dot_general | solution.py:585
  309.0 3.0 fusion.39
  312.0 11.1 %collective-permute-done.16 = bf16[128,1664]{1,0:T(8,128)(2,1)} collective-permute-done((bf16[128,1664]{1,0:T(8,128)(2,1)}, bf16[128,1664]{1,0:T(8,128)(2,1)}, u32[]{:S(2)}, u32[]{:S(2)}) %collective-permute-start.16) | collective-permute-done | bytes 426016 | tf_op jit(solution)/shard_map/ppermute | solution.py:590
  323.1 9.5 %collective-permute-done.18 = bf16[128,1664]{1,0:T(8,128)(2,1)} collective-permute-done((bf16[128,1664]{1,0:T(8,128)(2,1)}, bf16[128,1664]{1,0:T(8,128)(2,1)}, u32[]{:S(2)}, u32[]{:S(2)}) %collective-permute-start.18) | collective-permute-done | bytes 426016 | tf_op jit(solution)/shard_map/ppermute | solution.py:590
  343.7 2.8 collective-permute-done.20
  355.5 3.0 collective-permute-start.23
  (350 shorter events, 109.6 us)
Async XLA Ops:
  7.3 71.7 %all-gather.5.cloned.1.call-start = ((), (), s32[]{:S(2)}) async-start(), calls=%async_computation.4 | async-start | bytes 3833856 | tf_op jit(solution)/shard_map/all_gather | solution.py:687
  11.9 106.4 %all-gather.7.cloned.1.call-start = ((), (), s32[]{:S(2)}) async-start(), calls=%async_computation.5 | async-start | bytes 5308416 | tf_op jit(solution)/shard_map/all_gather | solution.py:693
  12.9 55.0 %all-to-all-start = ((bf16[4,256,1024]{2,1,0:T(8,128)(2,1)}), bf16[4,256,1024]{2,1,0:T(8,128)(2,1)S(1)}, u32[]{:S(2)}, u32[]{:S(2)}) async-start(bf16[4,256,1024]{2,1,0:T(8,128)(2,1)} %broadcast_in_dim.17), calls=%async_computation | async-start | bytes 4194304 | tf_op jit(solution)/shard_map/all_to_all | solution.py:594
  19.3 108.4 %all-gather.9.cloned.1.call-start = ((), (), s32[]{:S(2)}) async-start(), calls=%async_computation.6 | async-start | bytes 2359296 | tf_op jit(solution)/shard_map/all_gather | solution.py:724
  67.9 7.3 %collective-permute-start.2 = (bf16[128,256]{0,1:T(8,128)(2,1)S(1)}, bf16[128,256]{0,1:T(8,128)(2,1)S(1)}, u32[]{:S(2)}, u32[]{:S(2)}) collective-permute-start(bf16[128,256]{0,1:T(8,128)(2,1)S(1)} %bitcast.121), channel_id=1, source_target_pairs={{0,24},{8,16},{16,8},{24,0},{1,25},{9,17},{17,9},{25,1},{2,26},{10... | collective-permute-start | bytes 196616 | tf_op jit(solution)/shard_map/ppermute | solution.py:590
  69.0 6.4 %collective-permute-start.1 = (bf16[128,256]{0,1:T(8,128)(2,1)S(1)}, bf16[128,256]{0,1:T(8,128)(2,1)S(1)}, u32[]{:S(2)}, u32[]{:S(2)}) collective-permute-start(bf16[128,256]{0,1:T(8,128)(2,1)S(1)} %bitcast.122), channel_id=1, source_target_pairs={{0,16},{8,24},{16,0},{24,8},{1,17},{9,25},{17,1},{25,9},{2,18},{10... | collective-permute-start | bytes 196616 | tf_op jit(solution)/shard_map/ppermute | solution.py:590
  69.0 6.4 %collective-permute-start = (bf16[128,256]{0,1:T(8,128)(2,1)S(1)}, bf16[128,256]{0,1:T(8,128)(2,1)S(1)}, u32[]{:S(2)}, u32[]{:S(2)}) collective-permute-start(bf16[128,256]{0,1:T(8,128)(2,1)S(1)} %bitcast.123), channel_id=1, source_target_pairs={{0,8},{8,0},{16,24},{24,16},{1,9},{9,1},{17,25},{25,17},{2,10},{10... | collective-permute-start | bytes 196616 | tf_op jit(solution)/shard_map/ppermute | solution.py:590
  76.1 85.9 %all-gather.11.cloned.1.call-start = ((), (), s32[]{:S(2)}) async-start(), calls=%async_computation.7 | async-start | bytes 5308416 | tf_op jit(solution)/shard_map/all_gather | solution.py:735
  76.6 41.7 %collective-permute-start.3 = (bf16[256,1024]{1,0:T(8,128)(2,1)}, bf16[256,1024]{1,0:T(8,128)(2,1)}, u32[]{:S(2)}, u32[]{:S(2)}) collective-permute-start(bf16[256,1024]{1,0:T(8,128)(2,1)} %param.20), channel_id=1, source_target_pairs={{0,8},{8,0},{16,24},{24,16},{1,9},{9,1},{17,25},{25,17},{2,10},{10... | collective-permute-start | bytes 1572872 | tf_op jit(solution)/shard_map/ppermute | solution.py:590
  77.8 40.4 %collective-permute-start.4 = (bf16[128,2304]{0,1:T(8,128)(2,1)}, bf16[128,2304]{0,1:T(8,128)(2,1)}, u32[]{:S(2)}, u32[]{:S(2)}) collective-permute-start(bf16[128,2304]{0,1:T(8,128)(2,1)} %fusion.90), channel_id=1, source_target_pairs={{0,16},{8,24},{16,0},{24,8},{1,17},{9,25},{17,1},{25,9},{2,18},{10... | collective-permute-start | bytes 1769480 | tf_op jit(solution)/shard_map/ppermute | solution.py:590
  118.3 129.1 %reduce-scatter.3.cloned.1.call-start = ((), (), s32[]{:S(2)}) async-start(), calls=%async_computation.8 | async-start | bytes 5308416 | tf_op jit(solution)/shard_map/reduce_scatter | solution.py:793
  119.5 8.2 %collective-permute-start.7 = (bf16[256,256]{1,0:T(8,128)(2,1)}, bf16[256,256]{1,0:T(8,128)(2,1)}, u32[]{:S(2)}, u32[]{:S(2)}) collective-permute-start(bf16[256,256]{1,0:T(8,128)(2,1)} %get-tuple-element.309), channel_id=1, source_target_pairs={{0,24},{8,16},{16,8},{24,0},{1,25},{9,17},{17,9},{25,1},{2,26},{10... | collective-permute-start | bytes 393224 | tf_op jit(solution)/shard_map/ppermute | solution.py:590
  121.6 10.3 %collective-permute-start.6 = (bf16[256,256]{1,0:T(8,128)(2,1)}, bf16[256,256]{1,0:T(8,128)(2,1)}, u32[]{:S(2)}, u32[]{:S(2)}) collective-permute-start(bf16[256,256]{1,0:T(8,128)(2,1)} %get-tuple-element.310), channel_id=1, source_target_pairs={{0,16},{8,24},{16,0},{24,8},{1,17},{9,25},{17,1},{25,9},{2,18},{10... | collective-permute-start | bytes 393224 | tf_op jit(solution)/shard_map/ppermute | solution.py:590
  121.8 10.1 %collective-permute-start.5 = (bf16[256,256]{1,0:T(8,128)(2,1)}, bf16[256,256]{1,0:T(8,128)(2,1)}, u32[]{:S(2)}, u32[]{:S(2)}) collective-permute-start(bf16[256,256]{1,0:T(8,128)(2,1)} %get-tuple-element.311), channel_id=1, source_target_pairs={{0,8},{8,0},{16,24},{24,16},{1,9},{9,1},{17,25},{25,17},{2,10},{10... | collective-permute-start | bytes 393224 | tf_op jit(solution)/shard_map/ppermute | solution.py:590
  135.8 12.3 %collective-permute-start.8 = (bf16[256,1024]{1,0:T(8,128)(2,1)S(1)}, bf16[256,1024]{1,0:T(8,128)(2,1)S(1)}, u32[]{:S(2)}, u32[]{:S(2)}) collective-permute-start(bf16[256,1024]{1,0:T(8,128)(2,1)S(1)} %multiply_convert_fusion), channel_id=1, source_target_pairs={{0,8},{8,0},{16,24},{24,16},{1,9},{9,1},{17,25},{25,17},{2,10},{10... | collective-permute-start | bytes 1572872 | tf_op jit(solution)/shard_map/ppermute | solution.py:590
  179.1 14.3 %collective-permute-start.9 = (bf16[256,1024]{1,0:T(8,128)(2,1)}, bf16[256,1024]{1,0:T(8,128)(2,1)S(1)}, u32[]{:S(2)}, u32[]{:S(2)}) collective-permute-start(bf16[256,1024]{1,0:T(8,128)(2,1)} %fusion.40), channel_id=1, source_target_pairs={{0,8},{8,0},{16,24},{24,16},{1,9},{9,1},{17,25},{25,17},{2,10},{10... | collective-permute-start | bytes 1572872 | tf_op jit(solution)/shard_map/ppermute | solution.py:590
  193.4 142.5 %reduce-scatter.5.cloned.1.call-start = ((), (), s32[]{:S(2)}) async-start(), calls=%async_computation.9 | async-start | bytes 7667712 | tf_op jit(solution)/shard_map/reduce_scatter | solution.py:812
  200.6 12.5 %collective-permute-start.11 = (bf16[256,256]{1,0:T(8,128)(2,1)S(1)}, bf16[256,256]{1,0:T(8,128)(2,1)S(1)}, u32[]{:S(2)}, u32[]{:S(2)}) collective-permute-start(bf16[256,256]{1,0:T(8,128)(2,1)S(1)} %get-tuple-element.305), channel_id=1, source_target_pairs={{0,16},{8,24},{16,0},{24,8},{1,17},{9,25},{17,1},{25,9},{2,18},{10... | collective-permute-start | bytes 393224 | tf_op jit(solution)/shard_map/ppermute | solution.py:590
  203.1 6.6 %collective-permute-start.10 = (bf16[256,256]{1,0:T(8,128)(2,1)S(1)}, bf16[256,256]{1,0:T(8,128)(2,1)S(1)}, u32[]{:S(2)}, u32[]{:S(2)}) collective-permute-start(bf16[256,256]{1,0:T(8,128)(2,1)S(1)} %get-tuple-element.307), channel_id=1, source_target_pairs={{0,8},{8,0},{16,24},{24,16},{1,9},{9,1},{17,25},{25,17},{2,10},{10... | collective-permute-start | bytes 393224 | tf_op jit(solution)/shard_map/ppermute | solution.py:590
  204.6 8.5 %collective-permute-start.12 = (bf16[256,256]{1,0:T(8,128)(2,1)S(1)}, bf16[256,256]{1,0:T(8,128)(2,1)S(1)}, u32[]{:S(2)}, u32[]{:S(2)}) collective-permute-start(bf16[256,256]{1,0:T(8,128)(2,1)S(1)} %get-tuple-element.304), channel_id=1, source_target_pairs={{0,24},{8,16},{16,8},{24,0},{1,25},{9,17},{17,9},{25,1},{2,26},{10... | collective-permute-start | bytes 393224 | tf_op jit(solution)/shard_map/ppermute | solution.py:590
  247.4 28.9 %collective-permute-start.14 = (bf16[128,2304]{1,0:T(8,128)(2,1)}, bf16[128,2304]{1,0:T(8,128)(2,1)}, u32[]{:S(2)}, u32[]{:S(2)}) collective-permute-start(bf16[128,2304]{1,0:T(8,128)(2,1)} %reduce-scatter.3.cloned.1.call-done), channel_id=1, source_target_pairs={{0,16},{8,24},{16,0},{24,8},{1,17},{9,25},{17,1},{25,9},{2,18},{10... | collective-permute-start | bytes 1769480 | tf_op jit(solution)/shard_map/ppermute | solution.py:590
  249.9 24.4 %collective-permute-start.13 = (bf16[256,1024]{1,0:T(8,128)(2,1)}, bf16[256,1024]{1,0:T(8,128)(2,1)}, u32[]{:S(2)}, u32[]{:S(2)}) collective-permute-start(bf16[256,1024]{1,0:T(8,128)(2,1)} %fusion.38), channel_id=1, source_target_pairs={{0,8},{8,0},{16,24},{24,16},{1,9},{9,1},{17,25},{25,17},{2,10},{10... | collective-permute-start | bytes 1572872 | tf_op jit(solution)/shard_map/ppermute | solution.py:590
  287.4 7.6 %collective-permute-start.15 = (bf16[512,1664]{1,0:T(8,128)(2,1)}, bf16[512,1664]{1,0:T(8,128)(2,1)}, u32[]{:S(2)}, u32[]{:S(2)}) collective-permute-start(bf16[512,1664]{1,0:T(8,128)(2,1)} %convolution_convert_fusion.2), channel_id=1, source_target_pairs={{0,1},{1,0},{2,3},{3,2},{4,5},{5,4},{6,7},{7,6},{8,9},{9,8},{10,11... | collective-permute-start | bytes 5111816 | tf_op jit(solution)/shard_map/ppermute | solution.py:590
  289.5 61.3 %all-to-all-start.1 = ((bf16[4,256,1024]{2,1,0:T(8,128)(2,1)}), bf16[4,256,1024]{2,1,0:T(8,128)(2,1)}, u32[]{:S(2)}, u32[]{:S(2)}) async-start(bf16[4,256,1024]{2,1,0:T(8,128)(2,1)} %bitcast.104), calls=%async_computation.3 | async-start | bytes 4194304 | tf_op jit(solution)/shard_map/all_to_all | solution.py:594
  301.1 22.1 %collective-permute-start.16 = (bf16[128,1664]{1,0:T(8,128)(2,1)}, bf16[128,1664]{1,0:T(8,128)(2,1)}, u32[]{:S(2)}, u32[]{:S(2)}) collective-permute-start(bf16[128,1664]{1,0:T(8,128)(2,1)} %get-tuple-element.290), channel_id=1, source_target_pairs={{0,2},{1,3},{2,0},{3,1},{4,6},{5,7},{6,4},{7,5},{8,10},{9,11},{10,... | collective-permute-start | bytes 1277960 | tf_op jit(solution)/shard_map/ppermute | solution.py:590
  302.5 30.2 %collective-permute-start.18 = (bf16[128,1664]{1,0:T(8,128)(2,1)}, bf16[128,1664]{1,0:T(8,128)(2,1)}, u32[]{:S(2)}, u32[]{:S(2)}) collective-permute-start(bf16[128,1664]{1,0:T(8,128)(2,1)} %get-tuple-element.291), channel_id=1, source_target_pairs={{0,6},{1,7},{2,4},{3,5},{4,2},{5,3},{6,0},{7,1},{8,14},{9,15},{10,... | collective-permute-start | bytes 1277960 | tf_op jit(solution)/shard_map/ppermute | solution.py:590
  303.9 28.7 %collective-permute-start.17 = (bf16[128,1664]{1,0:T(8,128)(2,1)}, bf16[128,1664]{1,0:T(8,128)(2,1)}, u32[]{:S(2)}, u32[]{:S(2)}) collective-permute-start(bf16[128,1664]{1,0:T(8,128)(2,1)} %get-tuple-element.292), channel_id=1, source_target_pairs={{0,4},{1,5},{2,6},{3,7},{4,0},{5,1},{6,2},{7,3},{8,12},{9,13},{10,... | collective-permute-start | bytes 1277960 | tf_op jit(solution)/shard_map/ppermute | solution.py:590
  336.9 5.6 %collective-permute-start.19 = (f32[64,128]{1,0:T(8,128)S(1)}, f32[64,128]{1,0:T(8,128)S(1)}, u32[]{:S(2)}, u32[]{:S(2)}) collective-permute-start(f32[64,128]{1,0:T(8,128)S(1)} %pad_bitcast_fusion.1), channel_id=1, source_target_pairs={{0,1},{1,0},{2,3},{3,2},{4,5},{5,4},{6,7},{7,6},{8,9},{9,8},{10,11... | collective-permute-start | bytes 98312 | tf_op jit(solution)/shard_map/ppermute | solution.py:590
  338.4 8.7 %collective-permute-start.24 = (bf16[128,256]{1,0:T(8,128)(2,1)S(1)}, bf16[128,256]{1,0:T(8,128)(2,1)S(1)}, u32[]{:S(2)}, u32[]{:S(2)}) collective-permute-start(bf16[128,256]{1,0:T(8,128)(2,1)S(1)} %get-tuple-element.312), channel_id=1, source_target_pairs={{0,8},{8,0},{16,24},{24,16},{1,9},{9,1},{17,25},{25,17},{2,10},{10... | collective-permute-start | bytes 196616 | tf_op jit(solution)/shard_map/ppermute | solution.py:590
  340.1 7.0 %collective-permute-start.26 = (bf16[128,256]{1,0:T(8,128)(2,1)S(1)}, bf16[128,256]{1,0:T(8,128)(2,1)S(1)}, u32[]{:S(2)}, u32[]{:S(2)}) collective-permute-start(bf16[128,256]{1,0:T(8,128)(2,1)S(1)} %get-tuple-element.313), channel_id=1, source_target_pairs={{0,24},{8,16},{16,8},{24,0},{1,25},{9,17},{17,9},{25,1},{2,26},{10... | collective-permute-start | bytes 196616 | tf_op jit(solution)/shard_map/ppermute | solution.py:590
  342.5 6.7 %collective-permute-start.25 = (bf16[128,256]{1,0:T(8,128)(2,1)S(1)}, bf16[128,256]{1,0:T(8,128)(2,1)S(1)}, u32[]{:S(2)}, u32[]{:S(2)}) collective-permute-start(bf16[128,256]{1,0:T(8,128)(2,1)S(1)} %get-tuple-element.314), channel_id=1, source_target_pairs={{0,16},{8,24},{16,0},{24,8},{1,17},{9,25},{17,1},{25,9},{2,18},{10... | collective-permute-start | bytes 196616 | tf_op jit(solution)/shard_map/ppermute | solution.py:590
  355.5 7.7 %collective-permute-start.23 = (f32[184,128]{1,0:T(8,128)S(1)}, f32[184,128]{1,0:T(8,128)S(1)}, u32[]{:S(2)}, u32[]{:S(2)}) collective-permute-start(f32[184,128]{1,0:T(8,128)S(1)} %add.244), channel_id=1, source_target_pairs={{0,16},{8,24},{16,0},{24,8},{1,17},{9,25},{17,1},{25,9},{2,18},{10... | collective-permute-start | bytes 282632 | tf_op jit(solution)/shard_map/ppermute | solution.py:590
  (77 other events, 764.7 us)
Sparse Core Ops, SparseCore 0:
  12.0 36.1 all-gather.4
  50.1 39.7 all-gather.6
  92.3 28.1 all-gather.8
  122.3 39.7 all-gather.10
  193.5 53.8 reduce-scatter.2
  251.1 73.2 reduce-scatter.4
